TPU v7x, 256 devices: a whole 4x4x8 slice. The times are simulated.
256 devices in a mesh: gx: 16 (over z, y_lo), gy: 8 (over x, core), gz: 2 (over y_hi).
Axes of the slice: x: 4, y: 4 (y_hi: 2, y_lo: 2; y = y_hi * 2 + y_lo), z: 8, core: 2. Of those that a mesh axis runs over, the one named last changes fastest.
Arguments:
- state: float32 [128, 4, 256, 1024], P('gz', None, 'gx', 'gy'), may hold values from -6 to 6
- metric: float32 [256, 1024], P('gx', 'gy'), may hold values from 0.25 to 1.75
- couple: float32 [128, 4, 256, 1024], P('gz', None, 'gx', 'gy'), may hold values from 1 to 4000
- base: float32 [128, 4, 256, 1024], P('gz', None, 'gx', 'gy'), may hold values from 0.5 to 2
Outputs:
- new_state: float32 [128, 4, 256, 1024], P('gz', None, 'gx', 'gy')
All inputs are finite; a program needn't handle non-finite values.
Results may differ from a plain program's by a relative error of at most 0.0003.
Values sent between devices are 32-bit elements; how exact they have to be, the bound alone decides.
No kernel may reach another device: no remote copies, remote signals or barrier semaphores. Data moves between devices by JAX's collectives and lax.ppermute only.
A program may use at most 128 MiB of HBM per device.

v0:
```python
import jax
import jax.numpy as jnp
from jax import lax
from jax.sharding import PartitionSpec as P

step_dt = 0.5
sound_sq = 1.0
hyper_nu = 0.01


def with_halo(cells, sides, width, closed):
    for axis, dim in sides:
        count = lax.axis_size(axis)
        ends = count if closed else count - 1
        head = lax.slice_in_dim(cells, 0, width, axis=dim)
        tail = lax.slice_in_dim(cells, cells.shape[dim] - width, cells.shape[dim], axis=dim)
        cells = jnp.concatenate(
            [
                lax.ppermute(tail, axis, [(i, (i + 1) % count) for i in range(ends)]),
                cells,
                lax.ppermute(head, axis, [((i + 1) % count, i) for i in range(ends)]),
            ],
            axis=dim,
        )
    return cells


def laplace(padded):
    return (
        padded[:, 2:, 1:-1]
        + padded[:, :-2, 1:-1]
        + padded[:, 1:-1, 2:]
        + padded[:, 1:-1, :-2]
        - 4.0 * padded[:, 1:-1, 1:-1]
    )


def forward_pass(lower, middle, upper, values, start):

    def advance(carry, item):
        c_prev, d_prev = carry
        low, mid, high, value = item
        denom = mid - low * c_prev
        c_next = high / denom
        d_next = (value + low * d_prev) / denom
        return ((c_next, d_next), (c_next, d_next))

    final, (c_all, d_all) = lax.scan(advance, start, (lower, middle, upper, values), unroll=True)
    return (c_all, d_all)


def backward_pass(c_all, d_all, start):

    def retreat(x_next, item):
        c_here, d_here = item
        x_here = d_here + c_here * x_next
        return (x_here, x_here)

    final, x_all = lax.scan(retreat, start, (c_all, d_all), reverse=True, unroll=True)
    return x_all


def shards(state, metric, couple, base):
    levels = state.shape[0]
    width_x = state.shape[2]
    width_y = state.shape[3]
    wind_u = state[:, 0]
    wind_v = state[:, 1]
    wind_w = state[:, 2]
    pressure = state[:, 3]
    padded = with_halo(pressure, (("gx", 1),), 2, True)
    padded = with_halo(padded, (("gy", 2),), 2, False)
    new_u = wind_u - step_dt * 0.5 * metric * (padded[:, 3:-1, 2:-2] - padded[:, 1:-3, 2:-2])
    new_v = wind_v - step_dt * 0.5 * metric * (padded[:, 2:-2, 3:-1] - padded[:, 2:-2, 1:-3])
    outer_u = with_halo(new_u, (("gx", 1),), 1, True)
    outer_v = with_halo(new_v, (("gy", 2),), 1, False)
    diff_u = outer_u[:, 2:] - outer_u[:, :-2]
    diff_v = outer_v[:, :, 2:] - outer_v[:, :, :-2]
    divergence = 0.5 * metric * metric * (diff_u + diff_v)
    second = laplace(laplace(padded))
    new_p = pressure - step_dt * sound_sq * divergence - hyper_nu * second
    fields = jnp.stack([new_u, new_v, wind_w, new_p], axis=1)
    rows = 4 * width_x
    fields = fields.reshape(levels, rows, width_y)
    coupling = couple.reshape(levels, rows, width_y)
    weight = base.reshape(levels, rows, width_y)
    whole_f, whole_c, whole_w = (
        lax.all_to_all(fields, "gz", split_axis=1, concat_axis=0, tiled=True),
        lax.all_to_all(coupling, "gz", split_axis=1, concat_axis=0, tiled=True),
        lax.all_to_all(weight, "gz", split_axis=1, concat_axis=0, tiled=True),
    )
    total = whole_f.shape[0]
    level_ids = jnp.arange(total, dtype=jnp.int32)
    upper = jnp.where((level_ids < total - 1)[:, None, None], whole_c, jnp.float32(0.0))
    lower = jnp.concatenate([jnp.zeros_like(upper[:1]), upper[:-1]], axis=0)
    middle = whole_w + lower + upper
    values = whole_w * whole_f
    zeros = jnp.zeros(whole_f.shape[1:], jnp.float32)
    c_all, d_all = forward_pass(lower, middle, upper, values, (zeros, zeros))
    solved = backward_pass(c_all, d_all, zeros)
    result = lax.all_to_all(solved, "gz", split_axis=0, concat_axis=1, tiled=True)
    return result.reshape(levels, 4, width_x, width_y)


def solution(mesh):
    in_specs = (
        P("gz", None, "gx", "gy"),
        P("gx", "gy"),
        P("gz", None, "gx", "gy"),
        P("gz", None, "gx", "gy"),
    )
    out_specs = P("gz", None, "gx", "gy")
    return jax.shard_map(shards, mesh=mesh, in_specs=in_specs, out_specs=out_specs, check_vma=False)
```

profile of v0, /device:TPU:6, one launch (start us, length us, event | category | flops | bytes accessed | tf_op | source)
XLA Modules:
  0.0 140.4 jit_solution(8255906749251008813)
XLA Ops:
  0.0 2.2 %fusion.779 = (f32[64,1,16,128]{3,2,1,0:T(8,128)}, f32[64,16,128]{2,1,0:T(8,128)S(1)}) fusion(f32[64,4,16,128]{3,2,1,0:T(8,128)} %param.4), kind=kLoop, calls=%fused_computation.1198 | loop fusion | bytes 2097152 | tf_op jit(solution)/shard_map/slice | solution.py:69
  2.3 1.7 %collective-permute-start.1 = (f32[64,2,128]{2,1,0:T(2,128)S(1)}, f32[64,2,128]{2,1,0:T(2,128)S(1)}, u32[]{:S(2)}, u32[]{:S(2)}) collective-permute-start(f32[64,2,128]{2,1,0:T(2,128)S(1)} %get-tuple-element.334), channel_id=1, source_target_pairs={{0,16},{16,32},{32,48},{48,64},{64,80},{80,96},{96,112},{112,128},... | collective-permute-start | bytes 196616 | tf_op jit(solution)/shard_map/ppermute | solution.py:19
  3.9 5.4 %collective-permute-start = (f32[64,2,128]{2,1,0:T(2,128)S(1)}, f32[64,2,128]{2,1,0:T(2,128)S(1)}, u32[]{:S(2)}, u32[]{:S(2)}) collective-permute-start(f32[64,2,128]{2,1,0:T(2,128)S(1)} %get-tuple-element.335), channel_id=1, source_target_pairs={{16,0},{32,16},{48,32},{64,48},{80,64},{96,80},{112,96},{128,112},... | collective-permute-start | bytes 196616 | tf_op jit(solution)/shard_map/ppermute | solution.py:21
  9.3 2.5 %copy.40 = f32[64,4,16,128]{3,0,2,1:T(8,128)} copy(f32[64,4,16,128]{3,2,1,0:T(8,128)S(1)} %copy-done.4) | data formatting | bytes 4194304 | tf_op args[2]
  11.9 4.9 %all-to-all-start.2 = ((f32[64,64,128]{2,0,1:T(8,128)}), f32[64,64,128]{2,0,1:T(8,128)}, u32[]{:S(2)}, u32[]{:S(2)}) async-start(f32[64,64,128]{2,0,1:T(8,128)} %bitcast.19), calls=%async_computation.2 | async-start | bytes 4194304 | tf_op jit(solution)/shard_map/all_to_all | solution.py:89
  16.7 0.0 collective-permute-done.1
  16.7 0.1 pad_maximum_fusion.8
  16.9 0.0 copy-start.6
  16.9 0.3 fusion.780
  17.1 0.3 copy.31
  17.4 0.3 copy.29
  17.7 1.9 %collective-permute-start.2 = (f32[64,20,2]{0,2,1:T(2,128)S(1)}, f32[64,20,2]{0,2,1:T(2,128)S(1)}, u32[]{:S(2)}, u32[]{:S(2)}) collective-permute-start(f32[64,20,2]{0,2,1:T(2,128)S(1)} %copy.29), channel_id=1, source_target_pairs={{2,0},{4,2},{6,4},{8,6},{10,8},{12,10},{14,12},{3,1},{5,3},{7,5},{... | collective-permute-start | bytes 30728 | tf_op jit(solution)/shard_map/ppermute | solution.py:21
  19.6 2.4 %collective-permute-start.3 = (f32[64,20,2]{0,2,1:T(2,128)S(1)}, f32[64,20,2]{0,2,1:T(2,128)S(1)}, u32[]{:S(2)}, u32[]{:S(2)}) collective-permute-start(f32[64,20,2]{0,2,1:T(2,128)S(1)} %copy.31), channel_id=1, source_target_pairs={{0,2},{2,4},{4,6},{6,8},{8,10},{10,12},{12,14},{1,3},{3,5},{5,7},{... | collective-permute-start | bytes 30728 | tf_op jit(solution)/shard_map/ppermute | solution.py:19
  22.1 4.1 %copy.23 = f32[64,4,16,128]{3,0,2,1:T(8,128)} copy(f32[64,4,16,128]{3,2,1,0:T(8,128)} %param.7) | data formatting | bytes 4194304 | tf_op args[3]
  26.2 0.3 copy.32
  26.6 0.3 copy.30
  26.9 2.1 %fusion.18 = (f32[64,16,128]{2,1,0:T(8,128)S(1)}, f32[64,16,128]{2,1,0:T(8,128)S(1)}) fusion(f32[64,16,128]{2,1,0:T(8,128)S(1)} %get-tuple-element.327, f32[64,2,128]{2,1,0:T(2,128)S(1)} %collective-permute-done.1, f32[64,2,128]{2,1,0:T(2,128)S(1)} %collective-permute-done, f32[64,4,16,128]{3,2,1,0:T(8,128)} %param.4, f32[16,128]{1,0:T(8,128)S(1)} %get-tuple-element.337, ...), kind=kLoop, calls=%fused_computation.42 | loop fusion | flops 1835008 | bytes 2781184 | tf_op jit(solution)/shard_map/sub | solution.py:73
  29.1 2.0 %collective-permute-start.4 = (f32[64,1,128]{2,1,0:T(1,128)S(1)}, f32[64,1,128]{2,1,0:T(1,128)S(1)}, u32[]{:S(2)}, u32[]{:S(2)}) collective-permute-start(f32[64,1,128]{2,1,0:T(1,128)S(1)} %get-tuple-element.330), channel_id=1, source_target_pairs={{16,0},{32,16},{48,32},{64,48},{80,64},{96,80},{112,96},{128,112},... | collective-permute-start | bytes 98312 | tf_op jit(solution)/shard_map/ppermute | solution.py:21
  31.1 0.1 collective-permute-start.5
  31.2 13.0 %all-to-all-done.2 = f32[64,64,128]{2,0,1:T(8,128)} async-done(((f32[64,64,128]{2,0,1:T(8,128)}), f32[64,64,128]{2,0,1:T(8,128)}, u32[]{:S(2)}, u32[]{:S(2)}) %all-to-all-start.2) | async-done | bytes 2097184 | tf_op jit(solution)/shard_map/all_to_all | solution.py:89
  44.2 4.8 %all-to-all-start = ((f32[64,64,128]{2,0,1:T(8,128)}), f32[64,64,128]{2,0,1:T(8,128)}, u32[]{:S(2)}, u32[]{:S(2)}) async-start(f32[64,64,128]{2,0,1:T(8,128)} %bitcast.4070), calls=%async_computation | async-start | bytes 4194304 | tf_op jit(solution)/shard_map/all_to_all | solution.py:90
  49.0 0.2 fusion.782
  49.2 1.9 %collective-permute-start.6 = (f32[64,16,1]{2,1,0:T(8,128)S(1)}, f32[64,16,1]{2,1,0:T(8,128)S(1)}, u32[]{:S(2)}, u32[]{:S(2)}) collective-permute-start(f32[64,16,1]{2,1,0:T(8,128)S(1)} %get-tuple-element.332), channel_id=1, source_target_pairs={{2,0},{4,2},{6,4},{8,6},{10,8},{12,10},{14,12},{3,1},{5,3},{7,5},{... | collective-permute-start | bytes 12296 | tf_op jit(solution)/shard_map/ppermute | solution.py:21
  51.1 2.6 %collective-permute-start.7 = (f32[64,16,1]{2,1,0:T(8,128)S(1)}, f32[64,16,1]{2,1,0:T(8,128)S(1)}, u32[]{:S(2)}, u32[]{:S(2)}) collective-permute-start(f32[64,16,1]{2,1,0:T(8,128)S(1)} %get-tuple-element.333), channel_id=1, source_target_pairs={{0,2},{2,4},{4,6},{6,8},{8,10},{10,12},{12,14},{1,3},{3,5},{5,7},{... | collective-permute-start | bytes 12296 | tf_op jit(solution)/shard_map/ppermute | solution.py:19
  53.8 0.9 pad_maximum_fusion.7
  54.7 2.1 %fusion.1 = f32[64,18,130]{2,1,0:T(8,128)S(1)} fusion(f32[64,20,132]{2,1,0:T(8,128)S(1)} %pad_maximum_fusion.7, f32[64,20,2]{2,1,0:T(8,128)S(1)} %copy.32, f32[64,2,128]{2,1,0:T(2,128)S(1)} %collective-permute-done, f32[64,16,128]{2,1,0:T(8,128)S(1)} %get-tuple-element.327, f32[64,2,128]{2,1,0:T(2,128)S(1)} %collective-permute-done.1, f32[64,20,2]{2,1,0:T(8,128)S(1)} %copy.30), kind=kLoop, calls=%fused_computation.6 | loop fusion | flops 1647360 | bytes 3072000 | tf_op jit(solution)/shard_map/sub | solution.py:30
  56.8 1.0 collective-permute-done.6
  57.8 3.8 %collective-permute-done.7 = f32[64,16,1]{2,1,0:T(8,128)S(1)} collective-permute-done((f32[64,16,1]{2,1,0:T(8,128)S(1)}, f32[64,16,1]{2,1,0:T(8,128)S(1)}, u32[]{:S(2)}, u32[]{:S(2)}) %collective-permute-start.7) | collective-permute-done | bytes 4128 | tf_op jit(solution)/shard_map/ppermute | solution.py:19
  61.6 2.2 %fusion.7 = f32[64,1,16,128]{3,2,1,0:T(8,128)S(1)} fusion(f32[64,18,130]{2,1,0:T(8,128)S(1)} %fusion.1, f32[64,16,128]{2,1,0:T(8,128)S(1)} %get-tuple-element.323, f32[64,16,1]{2,1,0:T(8,128)S(1)} %collective-permute-done.7, f32[64,16,1]{2,1,0:T(8,128)S(1)} %collective-permute-done.6, f32[64,16,128]{2,1,0:T(8,128)S(1)} %get-tuple-element.322, ...), kind=kLoop, calls=%fused_computation.22 | loop fusion | flops 2228224 | bytes 4800512 | tf_op jit(solution)/shard_map/stack | solution.py:82
  63.8 0.1 pad_maximum_fusion
  64.0 2.5 %copy.37 = f32[64,64,128]{2,0,1:T(8,128)} copy(f32[64,64,128]{2,1,0:T(8,128)S(1)} %bitcast.4071) | data formatting | bytes 4194304 | tf_op jit(solution)/shard_map/reshape | solution.py:84
  66.5 7.7 %all-to-all-done = f32[64,64,128]{2,0,1:T(8,128)} async-done(((f32[64,64,128]{2,0,1:T(8,128)}), f32[64,64,128]{2,0,1:T(8,128)}, u32[]{:S(2)}, u32[]{:S(2)}) %all-to-all-start) | async-done | bytes 2097184 | tf_op jit(solution)/shard_map/all_to_all | solution.py:90
  74.2 5.0 %all-to-all-start.1 = ((f32[64,64,128]{2,0,1:T(8,128)}), f32[64,64,128]{2,0,1:T(8,128)}, u32[]{:S(2)}, u32[]{:S(2)}) async-start(f32[64,64,128]{2,0,1:T(8,128)} %copy.37), calls=%async_computation.1 | async-start | bytes 4194304 | tf_op jit(solution)/shard_map/all_to_all | solution.py:88
  79.2 2.8 %copy.42 = f32[2,64,32,128]{3,2,1,0:T(8,128)S(1)} copy(f32[2,64,32,128]{3,1,2,0:T(8,128)} %bitcast.22) | data formatting | bytes 4194304 | tf_op jit(solution)/shard_map/all_to_all | solution.py:89
  82.1 0.2 bitcast_select_fusion
  82.3 1.2 copy-done.2
  83.4 4.9 %copy.25 = f32[2,64,32,128]{3,2,1,0:T(8,128)} copy(f32[2,64,32,128]{3,1,2,0:T(8,128)} %bitcast.3) | data formatting | bytes 4194304 | tf_op jit(solution)/shard_map/all_to_all | solution.py:90
  88.4 14.8 %all-to-all-done.1 = f32[64,64,128]{2,0,1:T(8,128)} async-done(((f32[64,64,128]{2,0,1:T(8,128)}), f32[64,64,128]{2,0,1:T(8,128)}, u32[]{:S(2)}, u32[]{:S(2)}) %all-to-all-start.1) | async-done | bytes 2097184 | tf_op jit(solution)/shard_map/all_to_all | solution.py:88
  103.2 3.0 %copy.39 = f32[2,64,32,128]{3,2,1,0:T(8,128)S(1)} copy(f32[2,64,32,128]{3,1,2,0:T(8,128)} %bitcast.16) | data formatting | bytes 4194304 | tf_op jit(solution)/shard_map/all_to_all | solution.py:88
  106.2 2.6 %bitcast_multiply_fusion = (f32[128,32,128]{2,1,0:T(8,128)S(1)}, f32[128,32,128]{2,1,0:T(8,128)S(1)}) fusion(f32[2,64,32,128]{3,2,1,0:T(8,128)S(1)} %copy.39, f32[2,64,32,128]{3,2,1,0:T(8,128)} %copy.25, f32[127,32,128]{2,1,0:T(8,128)S(1)} %slice-done, f32[2,64,32,128]{3,2,1,0:T(8,128)S(1)} %copy-done.3, pred[128]{0:T(512)(128)(4,1)S(1)} %iota_compare_fusion), kind=kLoop, calls=%fused_computation.2 | loop fusion | flops 2097152 | bytes 12566656 | tf_op jit(solution)/shard_map/mul | solution.py:97
  108.8 0.3 fusion.433
  109.1 0.6 fusion.124
  109.7 0.2 fusion.321
  109.9 0.4 fusion.129
  110.3 0.3 fusion.30
  110.6 0.7 constant_dynamic-update-slice_fusion.127
  113.0 25.8 %all_to_all.69 = f32[128,32,128]{2,1,0:T(8,128)S(1)} all-to-all(f32[128,32,128]{2,1,0:T(8,128)S(1)} %constant_dynamic-update-slice_fusion), channel_id=1, replica_groups=mesh['gx'=16,'gy'=8,'gz'=2] {'gz'}, dimensions={0} | all-to-all | bytes 4194304 | tf_op jit(solution)/shard_map/all_to_all | solution.py:101
  138.8 1.5 %copy.43 = f32[64,2,32,128]{3,2,1,0:T(8,128)} copy(f32[64,2,32,128]{3,2,0,1:T(8,128)S(1)} %bitcast.4072) | data formatting | bytes 4194304 | tf_op jit(solution)/shard_map/all_to_all | solution.py:101
  (151 shorter events, 0.9 us)
Async XLA Ops:
  0.0 9.3 %copy-start.4 = (f32[64,4,16,128]{3,2,1,0:T(8,128)S(1)}, f32[64,4,16,128]{3,2,1,0:T(8,128)}, u32[]{:S(2)}) copy-start(f32[64,4,16,128]{3,2,1,0:T(8,128)} %param.6) | copy-start | bytes 6291460
  2.3 14.4 %collective-permute-start.1 = (f32[64,2,128]{2,1,0:T(2,128)S(1)}, f32[64,2,128]{2,1,0:T(2,128)S(1)}, u32[]{:S(2)}, u32[]{:S(2)}) collective-permute-start(f32[64,2,128]{2,1,0:T(2,128)S(1)} %get-tuple-element.334), channel_id=1, source_target_pairs={{0,16},{16,32},{32,48},{48,64},{64,80},{80,96},{96,112},{112,128},... | collective-permute-start | bytes 196616 | tf_op jit(solution)/shard_map/ppermute | solution.py:19
  3.9 12.8 %collective-permute-start = (f32[64,2,128]{2,1,0:T(2,128)S(1)}, f32[64,2,128]{2,1,0:T(2,128)S(1)}, u32[]{:S(2)}, u32[]{:S(2)}) collective-permute-start(f32[64,2,128]{2,1,0:T(2,128)S(1)} %get-tuple-element.335), channel_id=1, source_target_pairs={{16,0},{32,16},{48,32},{64,48},{80,64},{96,80},{112,96},{128,112},... | collective-permute-start | bytes 196616 | tf_op jit(solution)/shard_map/ppermute | solution.py:21
  11.9 32.3 %all-to-all-start.2 = ((f32[64,64,128]{2,0,1:T(8,128)}), f32[64,64,128]{2,0,1:T(8,128)}, u32[]{:S(2)}, u32[]{:S(2)}) async-start(f32[64,64,128]{2,0,1:T(8,128)} %bitcast.19), calls=%async_computation.2 | async-start | bytes 4194304 | tf_op jit(solution)/shard_map/all_to_all | solution.py:89
  16.9 5.2 %copy-start.6 = (f32[16,128]{1,0:T(8,128)S(1)}, f32[16,128]{1,0:T(8,128)}, u32[]{:S(2)}) copy-start(f32[16,128]{1,0:T(8,128)} %param.5) | copy-start | bytes 24580
  17.7 8.9 %collective-permute-start.2 = (f32[64,20,2]{0,2,1:T(2,128)S(1)}, f32[64,20,2]{0,2,1:T(2,128)S(1)}, u32[]{:S(2)}, u32[]{:S(2)}) collective-permute-start(f32[64,20,2]{0,2,1:T(2,128)S(1)} %copy.29), channel_id=1, source_target_pairs={{2,0},{4,2},{6,4},{8,6},{10,8},{12,10},{14,12},{3,1},{5,3},{7,5},{... | collective-permute-start | bytes 30728 | tf_op jit(solution)/shard_map/ppermute | solution.py:21
  19.6 6.6 %collective-permute-start.3 = (f32[64,20,2]{0,2,1:T(2,128)S(1)}, f32[64,20,2]{0,2,1:T(2,128)S(1)}, u32[]{:S(2)}, u32[]{:S(2)}) collective-permute-start(f32[64,20,2]{0,2,1:T(2,128)S(1)} %copy.31), channel_id=1, source_target_pairs={{0,2},{2,4},{4,6},{6,8},{8,10},{10,12},{12,14},{1,3},{3,5},{5,7},{... | collective-permute-start | bytes 30728 | tf_op jit(solution)/shard_map/ppermute | solution.py:19
  29.1 32.5 %collective-permute-start.4 = (f32[64,1,128]{2,1,0:T(1,128)S(1)}, f32[64,1,128]{2,1,0:T(1,128)S(1)}, u32[]{:S(2)}, u32[]{:S(2)}) collective-permute-start(f32[64,1,128]{2,1,0:T(1,128)S(1)} %get-tuple-element.330), channel_id=1, source_target_pairs={{16,0},{32,16},{48,32},{64,48},{80,64},{96,80},{112,96},{128,112},... | collective-permute-start | bytes 98312 | tf_op jit(solution)/shard_map/ppermute | solution.py:21
  31.1 30.5 %collective-permute-start.5 = (f32[64,1,128]{2,1,0:T(1,128)S(1)}, f32[64,1,128]{2,1,0:T(1,128)S(1)}, u32[]{:S(2)}, u32[]{:S(2)}) collective-permute-start(f32[64,1,128]{2,1,0:T(1,128)S(1)} %get-tuple-element.331), channel_id=1, source_target_pairs={{0,16},{16,32},{32,48},{48,64},{64,80},{80,96},{96,112},{112,128},... | collective-permute-start | bytes 98312 | tf_op jit(solution)/shard_map/ppermute | solution.py:19
  44.2 30.0 %all-to-all-start = ((f32[64,64,128]{2,0,1:T(8,128)}), f32[64,64,128]{2,0,1:T(8,128)}, u32[]{:S(2)}, u32[]{:S(2)}) async-start(f32[64,64,128]{2,0,1:T(8,128)} %bitcast.4070), calls=%async_computation | async-start | bytes 4194304 | tf_op jit(solution)/shard_map/all_to_all | solution.py:90
  49.2 8.6 %collective-permute-start.6 = (f32[64,16,1]{2,1,0:T(8,128)S(1)}, f32[64,16,1]{2,1,0:T(8,128)S(1)}, u32[]{:S(2)}, u32[]{:S(2)}) collective-permute-start(f32[64,16,1]{2,1,0:T(8,128)S(1)} %get-tuple-element.332), channel_id=1, source_target_pairs={{2,0},{4,2},{6,4},{8,6},{10,8},{12,10},{14,12},{3,1},{5,3},{7,5},{... | collective-permute-start | bytes 12296 | tf_op jit(solution)/shard_map/ppermute | solution.py:21
  51.1 10.5 %collective-permute-start.7 = (f32[64,16,1]{2,1,0:T(8,128)S(1)}, f32[64,16,1]{2,1,0:T(8,128)S(1)}, u32[]{:S(2)}, u32[]{:S(2)}) collective-permute-start(f32[64,16,1]{2,1,0:T(8,128)S(1)} %get-tuple-element.333), channel_id=1, source_target_pairs={{0,2},{2,4},{4,6},{6,8},{8,10},{10,12},{12,14},{1,3},{3,5},{5,7},{... | collective-permute-start | bytes 12296 | tf_op jit(solution)/shard_map/ppermute | solution.py:19
  61.6 2.2 %copy-start.5 = (f32[64,1,16,128]{3,2,1,0:T(8,128)S(1)}, f32[64,1,16,128]{3,2,1,0:T(8,128)}, u32[]{:S(2)}) copy-start(f32[64,1,16,128]{3,2,1,0:T(8,128)} %get-tuple-element.326) | copy-start | bytes 1572868
  74.2 29.1 %all-to-all-start.1 = ((f32[64,64,128]{2,0,1:T(8,128)}), f32[64,64,128]{2,0,1:T(8,128)}, u32[]{:S(2)}, u32[]{:S(2)}) async-start(f32[64,64,128]{2,0,1:T(8,128)} %copy.37), calls=%async_computation.1 | async-start | bytes 4194304 | tf_op jit(solution)/shard_map/all_to_all | solution.py:88
  82.0 1.4 copy-start.2
  83.4 4.9 %copy-start = (f32[128,32,128]{2,1,0:T(8,128)}, f32[128,32,128]{2,1,0:T(8,128)S(1)}, u32[]{:S(2)}) copy-start(f32[128,32,128]{2,1,0:T(8,128)S(1)} %bitcast_select_fusion) | copy-start | bytes 6291460
  103.2 3.0 %slice-start = ((f32[128,32,128]{2,1,0:T(8,128)}), f32[127,32,128]{2,1,0:T(8,128)S(1)}, s32[]{:S(2)}) async-start(f32[128,32,128]{2,1,0:T(8,128)} %copy-done), calls=%async_computation.4 | async-start | bytes 4161536 | tf_op jit(solution)/shard_map/slice | solution.py:95
  103.2 3.0 %copy-start.3 = (f32[2,64,32,128]{3,2,1,0:T(8,128)S(1)}, f32[2,64,32,128]{3,2,1,0:T(8,128)}, u32[]{:S(2)}) copy-start(f32[2,64,32,128]{3,2,1,0:T(8,128)} %copy-done.2) | copy-start | bytes 6291460
  106.2 2.6 %copy-start.1 = (f32[128,32,128]{2,1,0:T(8,128)S(1)}, f32[128,32,128]{2,1,0:T(8,128)}, u32[]{:S(2)}) copy-start(f32[128,32,128]{2,1,0:T(8,128)} %copy-done) | copy-start | bytes 6291460
where the time goes:
time: 141 us; the launch traced here: 140 us
  waiting for transfers between devices  40.4 us (29%)
  starting transfers between devices  32.7 us (23%)
  local copies, waits for them, and re-layouts  26.9 us (19%)
  blocking collectives  25.8 us (18%)
  other arithmetic  13.3 us (9%)
    all_to_all x1, blocking collectives, shards(): lax.all_to_all(solved, 'gz', split_axis=0, concat_axis=1, tiled=True)  25.8 us
    all_to_all x1, waiting for transfers between devices, shards(): lax.all_to_all(fields, 'gz', split_axis=1, concat_axis=0, tiled=True)  14.8 us
    all_to_all x1, waiting for transfers between devices, shards(): lax.all_to_all(coupling, 'gz', split_axis=1, concat_axis=0, tiled=True)  13 us
    ppermute x4, starting transfers between devices, with_halo(): lax.ppermute(head, axis, [((i + 1) % count, i) for i in range(ends)])  11.2 us
    unnamed x79, local copies, waits for them, and re-layouts  8.1 us
    all_to_all x1, waiting for transfers between devices, shards(): lax.all_to_all(weight, 'gz', split_axis=1, concat_axis=0, tiled=True)  7.65 us
    ppermute x4, starting transfers between devices, with_halo(): lax.ppermute(tail, axis, [(i, (i + 1) % count) for i in range(ends)])  6.76 us
    all_to_all x1, starting transfers between devices, shards(): lax.all_to_all(fields, 'gz', split_axis=1, concat_axis=0, tiled=True)  5.05 us
  transfers between devices with their start and end apart: 11, of which 5 were waited for; matrix products, arithmetic and copies ran while one was open for 19% of the time, Pallas kernels for 0%

commit v1 on v0

v1 whole, which is shorter than its diff:
```python
import functools

import jax
import jax.numpy as jnp
from jax import lax
from jax.experimental import pallas as pl
from jax.experimental.pallas import tpu as pltpu
from jax.sharding import PartitionSpec as P

step_dt = 0.5
sound_sq = 1.0
hyper_nu = 0.01

f32 = jnp.float32
ANY = pl.BlockSpec(memory_space=pl.ANY)
VM = pl.BlockSpec(memory_space=pltpu.VMEM)
LIMIT = 32 * 1024 * 1024


def loop(count, body, carry, unroll):
    assert count % unroll == 0

    def several(i, carry):
        for j in range(unroll):
            carry = body(i * unroll + j, carry)
        return carry

    return lax.fori_loop(0, count // unroll, several, carry)


def row_ids(rows):
    return lax.broadcasted_iota(jnp.int32, (rows, 128), 0)


def lane_ids(rows):
    return lax.broadcasted_iota(jnp.int32, (rows, 128), 1)


def order(levels):
    top = lax.axis_index("gz")
    sign = 1 - 2 * top
    return top, sign, top * (levels - 1), top * (levels - 2)


def load_and_pack_x(state, metric, up, low_side, high_side, sems):
    levels = up.shape[0]
    copies = [
        pltpu.make_async_copy(state.at[:, field], up.at[:, slot], sems.at[slot])
        for slot, field in ((0, 0), (1, 3))
    ]
    for copy in copies:
        copy.start()
    for row, out in ((0, low_side), (15, high_side)):
        out[3 * levels : 3 * levels + 8, :] = jnp.broadcast_to(metric[row : row + 1, :], (8, 128))
    for copy in copies:
        copy.wait()
    flat = up.reshape(levels * 32, 128)
    for out, near, far in ((low_side, 0, 1), (high_side, 15, 14)):
        for part, row in enumerate((16 + near, 16 + far, near)):
            for base in range(0, levels, 8):
                out[part * levels + base : part * levels + base + 8, :] = flat[
                    pl.ds(base * 32 + row, 8, stride=32), :
                ]


def block_of(rows):
    return lax.rem(lane_ids(rows) + 2, 128) // 4


def factor(state, couple, base, metric, up, vw, part_a, part_b, part_c, edges, resist, pair, weights, sems):
    levels = vw.shape[0]
    top, sign, first, link = order(levels)
    chunk = levels // 4
    wind = [
        pltpu.make_async_copy(state.at[:, 1 + slot], vw.at[:, slot], sems.at[8 + slot]) for slot in range(2)
    ]
    copies = []
    for j in range(4):
        at = pl.ds(top * (levels - chunk) + sign * (j * chunk), chunk)
        copies.append(
            [
                pltpu.make_async_copy(couple.at[at], pair.at[at], sems.at[2 * j]),
                pltpu.make_async_copy(base.at[at], weights.at[at], sems.at[2 * j + 1]),
            ]
        )
    for group in copies:
        for copy in group:
            copy.start()
    for copy in wind:
        copy.start()

    def step(k, carry):
        g, before = carry
        here = first + sign * k
        weight = weights[here]
        after = pair[link + sign * k]
        total = weight + before * g
        inverse = 1.0 / (total + after)
        part_a[here] = weight * inverse
        part_b[here] = before * inverse
        part_c[here] = after * inverse
        return total * inverse, after

    zeros = jnp.zeros((4, 16, 128), f32)
    carry = (zeros, zeros)
    for j in range(4):
        if j == 0:
            for copy in copies[0] + copies[1]:
                copy.wait()
        elif j < 3:
            for copy in copies[j + 1]:
                copy.wait()
        count = chunk if j < 3 else chunk - 1
        start = j * chunk
        if count % 4 == 0:
            carry = loop(count, lambda k, c: step(start + k, c), carry, 4)
        else:
            carry = loop(count, lambda k, c: step(start + k, c), carry, 3)
    g, before = carry
    here = first + sign * (levels - 1)
    weight = weights[here]
    inverse = 1.0 / (weight + before * g)
    part_a[here] = weight * inverse
    part_b[here] = before * inverse
    part_c[here] = inverse
    outward = jnp.where(top == 0, 1.0 / pair[levels - 1], zeros)
    resist[...] = inverse + outward

    for copy in wind:
        copy.wait()
    block = block_of(16)
    for half in range(2):

        def gather(i, carry):
            kept_p, kept_v = carry
            level = half * (levels // 2) + i
            mine = block == i
            kept_p = jnp.where(mine, pltpu.roll(up[level, 1], 4 * i, 1), kept_p)
            kept_v = jnp.where(mine, pltpu.roll(vw[level, 0], 4 * i, 1), kept_v)
            return kept_p, kept_v

        kept = jnp.zeros((16, 128), f32)
        kept_p, kept_v = loop(levels // 2, gather, (kept, kept), 4)
        edges[16 * half : 16 * half + 16, :] = kept_p
        edges[32 + 16 * half : 48 + 16 * half, :] = kept_v
    own = jnp.where(block == 0, metric[...], 0.0)
    for shift in (4, 8, 16, 32, 64):
        own = own + pltpu.roll(own, shift, 1)
    edges[64:80, :] = own


def pack_y(edges, low_halo, high_halo, out):
    levels = (low_halo.shape[0] - 8) // 3
    out[0:80, :] = edges[...]
    block = block_of(8)
    row = row_ids(8)
    kept = jnp.zeros((8, 128), f32)
    for half in range(2):

        def gather(i, kept):
            level = half * (levels // 2) + i
            low = jnp.broadcast_to(low_halo[pl.ds(level, 1), :], (8, 128))
            high = jnp.broadcast_to(high_halo[pl.ds(level, 1), :], (8, 128))
            both = pltpu.roll(jnp.where(row == 2 * half, low, high), 4 * i, 1)
            return jnp.where((block == i) & (row // 2 == half), both, kept)

        kept = loop(levels // 2, gather, kept, 4)
    out[80:88, :] = kept


def interior(up, vw, low_halo, high_halo, metric, part_a, part_b, partial, done):
    levels = up.shape[0]
    top, sign, first, link = order(levels)
    row = row_ids(16)
    lane = lane_ids(16)
    m = metric[...]
    slope = step_dt * 0.5 * m
    spread = 0.5 * step_dt * sound_sq * m * m
    slope_low = step_dt * 0.5 * low_halo[3 * levels : 3 * levels + 1, :]
    slope_high = step_dt * 0.5 * high_halo[3 * levels : 3 * levels + 1, :]

    def east(z, far=1):
        return jnp.where(lane >= 128 - far, 0.0, pltpu.roll(z, 128 - far, 1))

    def west(z, far=1):
        return jnp.where(lane < far, 0.0, pltpu.roll(z, far, 1))

    def step(k, carry):
        d_u, d_w = carry
        l = first + sign * k
        p = up[l, 1]
        u = up[l, 0]
        v = vw[l, 0]
        w = vw[l, 1]
        near_low = low_halo[pl.ds(l, 1), :]
        far_low = low_halo[pl.ds(levels + l, 1), :]
        u_low = low_halo[pl.ds(2 * levels + l, 1), :]
        near_high = high_halo[pl.ds(l, 1), :]
        far_high = high_halo[pl.ds(levels + l, 1), :]
        u_high = high_halo[pl.ds(2 * levels + l, 1), :]
        before = jnp.where(row == 0, near_low, pltpu.roll(p, 1, 0))
        after = jnp.where(row == 15, near_high, pltpu.roll(p, 15, 0))
        before2 = jnp.where(row == 0, far_low, pltpu.roll(before, 1, 0))
        after2 = jnp.where(row == 15, far_high, pltpu.roll(after, 15, 0))
        u1 = u - slope * (after - before)
        v1 = v - slope * (east(p) - west(p))
        u1_low = u_low - slope_low * (p[0:1] - far_low)
        u1_high = u_high - slope_high * (far_high - p[15:16])
        diff_u = jnp.where(row == 15, u1_high, pltpu.roll(u1, 15, 0)) - jnp.where(
            row == 0, u1_low, pltpu.roll(u1, 1, 0)
        )
        diff_v = east(v1) - west(v1)
        sides = before + after
        cross = 2.0 * sides - 8.0 * p
        second = (before2 + after2) + (east(p, 2) + west(p, 2)) + (east(cross) + west(cross)) - 8.0 * sides + 20.0 * p
        p1 = p - spread * (diff_u + diff_v) - hyper_nu * second
        partial[l, 0] = v1
        partial[l, 1] = p1
        d_u = part_a[l, 0] * u1 + part_b[l, 0] * d_u
        d_w = part_a[l, 2] * w + part_b[l, 2] * d_w
        done[l, 0] = d_u
        done[l, 1] = d_w
        return d_u, d_w

    zeros = jnp.zeros((16, 128), f32)
    loop(levels, step, (zeros, zeros), 4)


def finish_forward(partial, done, part_a, part_b, metric, edges, left, right, resist, solved, out, fix_v, fix_p):
    levels = partial.shape[0]
    top, sign, first, link = order(levels)
    lane = lane_ids(16)
    row = row_ids(16)
    place = lax.rem(lane + 2, 4)
    m = edges[64:80, :]
    slope = step_dt * 0.5 * m
    spread = 0.5 * step_dt * sound_sq * m * m
    slope_left = step_dt * 0.5 * left[64:80, :]
    slope_right = step_dt * 0.5 * right[64:80, :]

    def shift(z, by):
        return pltpu.roll(z, by % 128, 1)

    for half in range(2):
        at = 16 * half

        def cross(side):
            p = side[at : at + 16, :]
            low = side[80 + 2 * half : 81 + 2 * half, :]
            high = side[81 + 2 * half : 82 + 2 * half, :]
            before = jnp.where(row == 0, low, pltpu.roll(p, 1, 0))
            after = jnp.where(row == 15, high, pltpu.roll(p, 15, 0))
            return 2.0 * (before + after) - 8.0 * p

        p_own = edges[at : at + 16, :]
        p_left = left[at : at + 16, :]
        p_right = right[at : at + 16, :]
        v_left = left[32 + at : 48 + at, :]
        v_right = right[32 + at : 48 + at, :]
        second = (
            jnp.where(place >= 2, shift(p_left, 2), shift(p_right, -2))
            + jnp.where(place == 2, shift(cross(left), 1), 0.0)
            + jnp.where(place == 1, shift(cross(right), -1), 0.0)
        )
        own_v = jnp.where(
            place == 2, slope * shift(p_left, 1), jnp.where(place == 1, -slope * shift(p_right, -1), 0.0)
        )
        v1_left = v_left - slope_left * (shift(p_own, -1) - shift(p_left, 1))
        v1_right = v_right - slope_right * (shift(p_right, -1) - shift(p_own, 1))
        diff_v = jnp.where(
            place == 2,
            -shift(v1_left, 1),
            jnp.where(place == 3, -shift(own_v, 1), jnp.where(place == 1, shift(v1_right, -1), shift(own_v, -1))),
        )
        fix_v[half] = own_v
        fix_p[half] = -spread * diff_v - hyper_nu * second

    edge = (lane >= 126) | (lane < 2)

    def step(k, carry):
        d_v, d_p = carry
        l = first + sign * k
        half = l // (levels // 2)
        back = lax.rem(128 - 4 * lax.rem(l, levels // 2), 128)
        v1 = partial[l, 0] + jnp.where(edge, pltpu.roll(fix_v[half], back, 1), 0.0)
        p1 = partial[l, 1] + jnp.where(edge, pltpu.roll(fix_p[half], back, 1), 0.0)
        d_v = part_a[l, 1] * v1 + part_b[l, 1] * d_v
        d_p = part_a[l, 3] * p1 + part_b[l, 3] * d_p
        solved[l, 0] = d_v
        solved[l, 1] = d_p
        return d_v, d_p

    zeros = jnp.zeros((16, 128), f32)
    d_v, d_p = loop(levels, step, (zeros, zeros), 4)
    last = first + sign * (levels - 1)
    out[0, 0] = done[last, 0]
    out[0, 1] = d_v
    out[0, 2] = done[last, 1]
    out[0, 3] = d_p
    out[1] = resist[...]


def back_substitute(done, solved, part_c, mine, other, out, x_ref, sems):
    levels = done.shape[0]
    top, sign, first, link = order(levels)
    last = first + sign * (levels - 1)
    x = mine[0] + (other[0] - mine[0]) * (part_c[last] / (mine[1] + other[1]))
    x_ref[last] = x
    chunk = levels // 4
    copies = []

    def step(k, x):
        l = last - sign * k
        c = part_c[l]
        parts = []
        for field in range(4):
            d = (done, solved)[field % 2][l, field // 2]
            parts.append(d + c[field] * x[field])
        x = jnp.stack(parts)
        x_ref[l] = x
        return x

    for j in range(4):
        start = j * chunk + (j == 0)
        count = chunk - (j == 0)
        x = loop(count, lambda k, x: step(start + k, x), x, 4 if count % 4 == 0 else 3)
        at = pl.ds((1 - top) * (levels - chunk) - sign * (j * chunk), chunk)
        copy = pltpu.make_async_copy(x_ref.at[at], out.at[at], sems.at[j])
        copy.start()
        copies.append(copy)
    for copy in copies:
        copy.wait()


def near(shape):
    return pltpu.VMEM(shape, f32)


def plain(shape):
    return jax.ShapeDtypeStruct(shape, f32)


def call(body, ins, outs, scratch, cost=0, name=None):
    def run(*args):
        return pl.pallas_call(
            body,
            in_specs=ins,
            out_specs=[s for s, _ in outs],
            out_shape=[o for _, o in outs],
            scratch_shapes=scratch,
            name=name,
            cost_estimate=pl.CostEstimate(flops=cost, bytes_accessed=cost, transcendentals=0) if cost else None,
            compiler_params=pltpu.CompilerParams(vmem_limit_bytes=LIMIT),
        )(*args)

    return run


def shards(state, metric, couple, base):
    levels = state.shape[0]
    nx, ny = lax.axis_size("gx"), lax.axis_size("gy")
    dma = pltpu.SemaphoreType.DMA
    edge_rows = 3 * levels + 8
    full = (levels, 4, 16, 128)
    two = (levels, 2, 16, 128)

    up, low_side, high_side = call(
        load_and_pack_x,
        [ANY, VM],
        [(VM, near(two)), (VM, plain((edge_rows, 128))), (VM, plain((edge_rows, 128)))],
        [dma((2,))],
        name="load_and_pack_x",
    )(state, metric)
    low_halo = lax.ppermute(high_side, "gx", [(i, (i + 1) % nx) for i in range(nx)])
    high_halo = lax.ppermute(low_side, "gx", [((i + 1) % nx, i) for i in range(nx)])

    vw, part_a, part_b, part_c, edges, resist = call(
        factor,
        [ANY, ANY, ANY, VM, VM],
        [
            (VM, near(two)),
            (VM, near(full)),
            (VM, near(full)),
            (VM, near(full)),
            (VM, near((80, 128))),
            (VM, near((4, 16, 128))),
        ],
        [pltpu.VMEM(full, f32), pltpu.VMEM(full, f32), dma((10,))],
        cost=8 * 1024 * 1024,
        name="factor",
    )(state, couple, base, metric, up)

    packed = call(
        pack_y, [VM, VM, VM], [(VM, plain((88, 128)))], [], name="pack_y"
    )(edges, low_halo, high_halo)[0]
    left = lax.ppermute(packed, "gy", [(i, i + 1) for i in range(ny - 1)])
    right = lax.ppermute(packed, "gy", [(i + 1, i) for i in range(ny - 1)])

    partial, done = call(
        interior,
        [VM] * 7,
        [(VM, near(two)), (VM, near(two))],
        [],
        cost=8 * 1024 * 1024,
        name="interior",
    )(up, vw, low_halo, high_halo, metric, part_a, part_b)

    solved, mine = call(
        finish_forward,
        [VM] * 9,
        [(VM, near(two)), (VM, plain((2, 4, 16, 128)))],
        [pltpu.VMEM((2, 16, 128), f32), pltpu.VMEM((2, 16, 128), f32)],
        name="finish_forward",
    )(partial, done, part_a, part_b, metric, packed, left, right, resist)
    other = lax.ppermute(mine, "gz", [(0, 1), (1, 0)])

    return call(
        back_substitute,
        [VM] * 5,
        [(ANY, plain(full))],
        [pltpu.VMEM(full, f32), dma((4,))],
        name="back_substitute",
    )(done, solved, part_c, mine, other)[0]


def solution(mesh):
    in_specs = (
        P("gz", None, "gx", "gy"),
        P("gx", "gy"),
        P("gz", None, "gx", "gy"),
        P("gz", None, "gx", "gy"),
    )
    out_specs = P("gz", None, "gx", "gy")
    return jax.shard_map(shards, mesh=mesh, in_specs=in_specs, out_specs=out_specs, check_vma=False)
```

time: 141 us -> 33.7 us (0.24)
  the two profiles are of different devices: /device:TPU:6 before, /device:TPU:1 now
where the time goes in v1:
time: 33.7 us; the launch traced here: 33.5 us
  starting transfers between devices  16.2 us (48%)
  Pallas kernels  10.6 us (31%)
  local copies, waits for them, and re-layouts  3.88 us (12%)
  waiting for transfers between devices  2.72 us (8%)
    pallas_call x6, Pallas kernels, run(): pl.pallas_call(body, in_specs=ins, out_specs=[s for s, _ in outs], out_sh...  10.6 us
    ppermute x1, starting transfers between devices, shards(): lax.ppermute(low_side, 'gx', [((i + 1) % nx, i) for i in range(nx)])  5.38 us
    unnamed x8, local copies, waits for them, and re-layouts  3.88 us
    ppermute x1, starting transfers between devices, shards(): left = lax.ppermute(packed, 'gy', [(i, i + 1) for i in range(ny - 1)])  3.02 us
    ppermute x1, starting transfers between devices, shards(): right = lax.ppermute(packed, 'gy', [(i + 1, i) for i in range(ny - 1)])  2.85 us
    ppermute x1, waiting for transfers between devices, shards(): other = lax.ppermute(mine, 'gz', [(0, 1), (1, 0)])  2.71 us
    ppermute x1, starting transfers between devices, shards(): other = lax.ppermute(mine, 'gz', [(0, 1), (1, 0)])  2.71 us
    ppermute x1, starting transfers between devices, shards(): lax.ppermute(high_side, 'gx', [(i, (i + 1) % nx) for i in range(nx)])  2.2 us
  transfers between devices with their start and end apart: 5, of which 1 were waited for; matrix products, arithmetic and copies ran while one was open for 0% of the time, Pallas kernels for 18%

profile of v1, /device:TPU:1, one launch (start us, length us, event | category | flops | bytes accessed | tf_op | source)
XLA Modules:
  0.0 33.5 jit_solution(11582587236444396569)
XLA Ops:
  0.0 0.0 copy-start
  0.0 1.6 %copy-done = f32[64,4,16,128]{3,2,1,0:T(8,128)S(1)} copy-done((f32[64,4,16,128]{3,2,1,0:T(8,128)S(1)}, f32[64,4,16,128]{3,2,1,0:T(8,128)}, u32[]{:S(2)}) %copy-start) | copy-done | bytes 2097176
  1.6 0.0 copy-start.3
  1.6 0.7 %copy-done.3 = f32[16,128]{1,0:T(8,128)S(1)} copy-done((f32[16,128]{1,0:T(8,128)S(1)}, f32[16,128]{1,0:T(8,128)}, u32[]{:S(2)}) %copy-start.3) | copy-done | bytes 8216
  2.3 0.0 copy-start.1
  2.3 0.3 load_and_pack_x.1
  2.6 2.2 %collective-permute-start = (f32[200,128]{1,0:T(8,128)S(1)}, f32[200,128]{1,0:T(8,128)S(1)}, u32[]{:S(2)}, u32[]{:S(2)}) collective-permute-start(f32[200,128]{1,0:T(8,128)S(1)} %get-tuple-element.20), channel_id=1, source_target_pairs={{0,16},{16,32},{32,48},{48,64},{64,80},{80,96},{96,112},{112,128},... | collective-permute-start | bytes 307208 | tf_op jit(solution)/shard_map/ppermute | solution.py:374
  4.8 5.4 %collective-permute-start.1 = (f32[200,128]{1,0:T(8,128)S(1)}, f32[200,128]{1,0:T(8,128)S(1)}, u32[]{:S(2)}, u32[]{:S(2)}) collective-permute-start(f32[200,128]{1,0:T(8,128)S(1)} %get-tuple-element.21), channel_id=1, source_target_pairs={{16,0},{32,16},{48,32},{64,48},{80,64},{96,80},{112,96},{128,112},... | collective-permute-start | bytes 307208 | tf_op jit(solution)/shard_map/ppermute | solution.py:375
  10.2 0.0 copy-done.1
  10.2 0.0 copy-start.2
  10.2 1.6 %copy-done.2 = f32[64,4,16,128]{3,2,1,0:T(8,128)S(1)} copy-done((f32[64,4,16,128]{3,2,1,0:T(8,128)S(1)}, f32[64,4,16,128]{3,2,1,0:T(8,128)}, u32[]{:S(2)}) %copy-start.2) | copy-done | bytes 2097176
  11.8 3.2 %factor.1 = (f32[64,2,16,128]{3,2,1,0:T(8,128)S(1)}, f32[64,4,16,128]{3,2,1,0:T(8,128)S(1)}, f32[64,4,16,128]{3,2,1,0:T(8,128)S(1)}, f32[64,4,16,128]{3,2,1,0:T(...) custom-call(f32[64,4,16,128]{3,2,1,0:T(8,128)S(1)} %copy-done, f32[64,4,16,128]{3,2,1,0:T(8,128)S(1)} %copy-done.1, ...), custom_call_target="tpu_custom_call" | custom-call | flops 8388608 | bytes 8388608 | tf_op jit(solution)/shard_map/factor/pallas_call | solution.py:345
  15.0 0.0 collective-permute-done.low_halo
  15.0 0.0 collective-permute-done.1.high_halo
  15.0 1.2 %pack_y.1.edges = f32[88,128]{1,0:T(8,128)S(1)} custom-call(f32[80,128]{1,0:T(8,128)S(1)} %get-tuple-element.26.edges, f32[200,128]{1,0:T(8,128)S(1)} %collective-permute-done.low_halo, f32[200,128]{1,0:T(8,128)S(1)} %collective-permute-done.1.high_halo), custom_call_target="tpu_custom_call" | custom-call | tf_op jit(solution)/shard_map/pack_y/pallas_call | solution.py:345
  16.2 2.9 %collective-permute-start.3 = (f32[88,128]{1,0:T(8,128)S(1)}, f32[88,128]{1,0:T(8,128)S(1)}, u32[]{:S(2)}, u32[]{:S(2)}) collective-permute-start(f32[88,128]{1,0:T(8,128)S(1)} %pack_y.1.edges), channel_id=1, source_target_pairs={{2,0},{4,2},{6,4},{8,6},{10,8},{12,10},{14,12},{3,1},{5,3},{7,5},{... | collective-permute-start | bytes 135176 | tf_op jit(solution)/shard_map/ppermute | solution.py:397
  19.1 3.0 %collective-permute-start.2 = (f32[88,128]{1,0:T(8,128)S(1)}, f32[88,128]{1,0:T(8,128)S(1)}, u32[]{:S(2)}, u32[]{:S(2)}) collective-permute-start(f32[88,128]{1,0:T(8,128)S(1)} %pack_y.1.edges), channel_id=1, source_target_pairs={{0,2},{2,4},{4,6},{6,8},{8,10},{10,12},{12,14},{1,3},{3,5},{5,7},{... | collective-permute-start | bytes 135176 | tf_op jit(solution)/shard_map/ppermute | solution.py:396
  22.1 2.7 %interior.1 = (f32[64,2,16,128]{3,2,1,0:T(8,128)S(1)}, f32[64,2,16,128]{3,2,1,0:T(8,128)S(1)}) custom-call(f32[64,2,16,128]{3,2,1,0:T(8,128)S(1)} %get-tuple-element.18.up, f32[64,2,16,128]{3,2,1,0:T(8,128)S(1)} %get-tuple-element.19.vw, f32[200,128]{1,0:T(8,128)S(1)} %collective-permute-done.low_halo, f32[200,128]{1,0:T(8,128)S(1)} %collective-permute-done.1.high_halo, ...), custom_call_target="tpu_custom_call" | custom-call | flops 8388608 | bytes 8388608 | tf_op jit(solution)/shard_map/interior/pallas_call | solution.py:345
  24.8 0.0 collective-permute-done.3.right
  24.8 0.0 collective-permute-done.2.left
  24.9 1.8 %finish_forward.1 = (f32[64,2,16,128]{3,2,1,0:T(8,128)S(1)}, f32[2,4,16,128]{3,2,1,0:T(8,128)S(1)}) custom-call(f32[64,2,16,128]{3,2,1,0:T(8,128)S(1)} %get-tuple-element.25.partial, f32[64,2,16,128]{3,2,1,0:T(8,128)S(1)} %get-tuple-element.24.done, f32[64,4,16,128]{3,2,1,0:T(8,128)S(1)} %get-tuple-element.22.part_a, ...), custom_call_target="tpu_custom_call" | custom-call | tf_op jit(solution)/shard_map/finish_forward/pallas_call | solution.py:345
  26.6 2.7 %collective-permute-start.4 = (f32[2,4,16,128]{3,2,1,0:T(8,128)S(1)}, f32[2,4,16,128]{3,2,1,0:T(8,128)S(1)}, u32[]{:S(2)}, u32[]{:S(2)}) collective-permute-start(f32[2,4,16,128]{3,2,1,0:T(8,128)S(1)} %get-tuple-element.30.mine), channel_id=1, source_target_pairs={{0,1},{1,0},{2,3},{3,2},{4,5},{5,4},{6,7},{7,6},{8,9},{9,8},{10,11... | collective-permute-start | bytes 196616 | tf_op jit(solution)/shard_map/ppermute | solution.py:415
  29.3 2.7 %collective-permute-done.4.other = f32[2,4,16,128]{3,2,1,0:T(8,128)S(1)} collective-permute-done((f32[2,4,16,128]{3,2,1,0:T(8,128)S(1)}, f32[2,4,16,128]{3,2,1,0:T(8,128)S(1)}, u32[]{:S(2)}, u32[]{:S(2)}) %collective-permute-start.4) | collective-permute-done | bytes 65568 | tf_op jit(solution)/shard_map/ppermute | solution.py:415
  32.1 1.4 %back_substitute.1 = f32[64,4,16,128]{3,2,1,0:T(8,128)} custom-call(f32[64,2,16,128]{3,2,1,0:T(8,128)S(1)} %get-tuple-element.24.done, f32[64,2,16,128]{3,2,1,0:T(8,128)S(1)} %get-tuple-element.28.solved, f32[64,4,16,128]{3,2,1,0:T(8,128)S(1)} %get-tuple-element.29.part_c, f32[2,4,16,128]{3,2,1,0:T(8,128)S(1)} %get-tuple-element.30.mine, ...), custom_call_target="tpu_custom_call" | custom-call | tf_op jit(solution)/shard_map/back_substitute/pallas_call | solution.py:345
Async XLA Ops:
  0.0 1.6 %copy-start = (f32[64,4,16,128]{3,2,1,0:T(8,128)S(1)}, f32[64,4,16,128]{3,2,1,0:T(8,128)}, u32[]{:S(2)}) copy-start(f32[64,4,16,128]{3,2,1,0:T(8,128)} %state.3) | copy-start | bytes 6291460
  1.6 0.7 %copy-start.3 = (f32[16,128]{1,0:T(8,128)S(1)}, f32[16,128]{1,0:T(8,128)}, u32[]{:S(2)}) copy-start(f32[16,128]{1,0:T(8,128)} %metric.7) | copy-start | bytes 24580
  2.3 7.9 %copy-start.1 = (f32[64,4,16,128]{3,2,1,0:T(8,128)S(1)}, f32[64,4,16,128]{3,2,1,0:T(8,128)}, u32[]{:S(2)}) copy-start(f32[64,4,16,128]{3,2,1,0:T(8,128)} %couple.1) | copy-start | bytes 6291460
  2.6 12.4 %collective-permute-start = (f32[200,128]{1,0:T(8,128)S(1)}, f32[200,128]{1,0:T(8,128)S(1)}, u32[]{:S(2)}, u32[]{:S(2)}) collective-permute-start(f32[200,128]{1,0:T(8,128)S(1)} %get-tuple-element.20), channel_id=1, source_target_pairs={{0,16},{16,32},{32,48},{48,64},{64,80},{80,96},{96,112},{112,128},... | collective-permute-start | bytes 307208 | tf_op jit(solution)/shard_map/ppermute | solution.py:374
  4.8 10.2 %collective-permute-start.1 = (f32[200,128]{1,0:T(8,128)S(1)}, f32[200,128]{1,0:T(8,128)S(1)}, u32[]{:S(2)}, u32[]{:S(2)}) collective-permute-start(f32[200,128]{1,0:T(8,128)S(1)} %get-tuple-element.21), channel_id=1, source_target_pairs={{16,0},{32,16},{48,32},{64,48},{80,64},{96,80},{112,96},{128,112},... | collective-permute-start | bytes 307208 | tf_op jit(solution)/shard_map/ppermute | solution.py:375
  10.2 1.6 %copy-start.2 = (f32[64,4,16,128]{3,2,1,0:T(8,128)S(1)}, f32[64,4,16,128]{3,2,1,0:T(8,128)}, u32[]{:S(2)}) copy-start(f32[64,4,16,128]{3,2,1,0:T(8,128)} %base.1) | copy-start | bytes 6291460
  16.2 8.6 %collective-permute-start.3 = (f32[88,128]{1,0:T(8,128)S(1)}, f32[88,128]{1,0:T(8,128)S(1)}, u32[]{:S(2)}, u32[]{:S(2)}) collective-permute-start(f32[88,128]{1,0:T(8,128)S(1)} %pack_y.1.edges), channel_id=1, source_target_pairs={{2,0},{4,2},{6,4},{8,6},{10,8},{12,10},{14,12},{3,1},{5,3},{7,5},{... | collective-permute-start | bytes 135176 | tf_op jit(solution)/shard_map/ppermute | solution.py:397
  19.1 5.8 %collective-permute-start.2 = (f32[88,128]{1,0:T(8,128)S(1)}, f32[88,128]{1,0:T(8,128)S(1)}, u32[]{:S(2)}, u32[]{:S(2)}) collective-permute-start(f32[88,128]{1,0:T(8,128)S(1)} %pack_y.1.edges), channel_id=1, source_target_pairs={{0,2},{2,4},{4,6},{6,8},{8,10},{10,12},{12,14},{1,3},{3,5},{5,7},{... | collective-permute-start | bytes 135176 | tf_op jit(solution)/shard_map/ppermute | solution.py:396
  26.6 5.4 %collective-permute-start.4 = (f32[2,4,16,128]{3,2,1,0:T(8,128)S(1)}, f32[2,4,16,128]{3,2,1,0:T(8,128)S(1)}, u32[]{:S(2)}, u32[]{:S(2)}) collective-permute-start(f32[2,4,16,128]{3,2,1,0:T(8,128)S(1)} %get-tuple-element.30.mine), channel_id=1, source_target_pairs={{0,1},{1,0},{2,3},{3,2},{4,5},{5,4},{6,7},{7,6},{8,9},{9,8},{10,11... | collective-permute-start | bytes 196616 | tf_op jit(solution)/shard_map/ppermute | solution.py:415

commit v2 on v1

v2 whole, which is shorter than its diff:
```python
import functools

import jax
import jax.numpy as jnp
from jax import lax
from jax.experimental import pallas as pl
from jax.experimental.pallas import tpu as pltpu
from jax.sharding import PartitionSpec as P

step_dt = 0.5
sound_sq = 1.0
hyper_nu = 0.01

f32 = jnp.float32
HB = pl.BlockSpec(memory_space=pltpu.HBM)
VM = pl.BlockSpec(memory_space=pltpu.VMEM)
LIMIT = 32 * 1024 * 1024


def loop(count, body, carry, unroll):
    assert count % unroll == 0

    def several(i, carry):
        for j in range(unroll):
            carry = body(i * unroll + j, carry)
        return carry

    return lax.fori_loop(0, count // unroll, several, carry)


def row_ids(rows):
    return lax.broadcasted_iota(jnp.int32, (rows, 128), 0)


def lane_ids(rows):
    return lax.broadcasted_iota(jnp.int32, (rows, 128), 1)


def order(levels):
    top = lax.axis_index("gz")
    sign = 1 - 2 * top
    return top, sign, top * (levels - 1), top * (levels - 2)


def pack_x(state, metric, low_side, high_side, sems):
    levels = state.shape[0]
    copies = []
    for out, rows in ((low_side, (0, 1, 0)), (high_side, (15, 14, 15))):
        for part, (field, row) in enumerate(zip((3, 3, 0), rows)):
            copies.append((state.at[:, field, row], out.at[pl.ds(part * levels, levels)]))
        copies.append((metric.at[pl.ds(rows[0], 1)], out.at[pl.ds(3 * levels, 1)]))
    copies = [pltpu.make_async_copy(src, dst, sems.at[i]) for i, (src, dst) in enumerate(copies)]
    for copy in copies:
        copy.start()
    for copy in copies:
        copy.wait()


def block_of(rows):
    return lax.rem(lane_ids(rows) + 2, 128) // 4


def factor(state, couple, base, metric, fields, own_metric, part_a, part_b, part_c, edges, resist, pair, weights, sems):
    levels = fields.shape[0]
    top, sign, first, link = order(levels)
    chunk = levels // 4
    early = [
        pltpu.make_async_copy(state.at[:, field], fields.at[:, field], sems.at[8 + i]) for i, field in enumerate((3, 1))
    ]
    early.append(pltpu.make_async_copy(metric, own_metric, sems.at[10]))
    late = [
        pltpu.make_async_copy(state.at[:, field], fields.at[:, field], sems.at[11 + i]) for i, field in enumerate((0, 2))
    ]
    copies = []
    for j in range(4):
        at = pl.ds(top * (levels - chunk) + sign * (j * chunk), chunk)
        copies.append(
            [
                pltpu.make_async_copy(couple.at[at], pair.at[at], sems.at[2 * j]),
                pltpu.make_async_copy(base.at[at], weights.at[at], sems.at[2 * j + 1]),
            ]
        )
    for copy in early + [copy for group in copies for copy in group] + late:
        copy.start()

    for copy in early:
        copy.wait()
    block = block_of(16)
    for half in range(2):

        def gather(i, carry):
            kept_p, kept_v = carry
            moved = []
            for j in range(16):
                at = 16 * i + j
                level = half * (levels // 2) + at
                moved.append(
                    (block == at, pltpu.roll(fields[level, 3], 4 * at, 1), pltpu.roll(fields[level, 1], 4 * at, 1))
                )
            for mine, p, v in moved:
                kept_p = jnp.where(mine, p, kept_p)
                kept_v = jnp.where(mine, v, kept_v)
            return kept_p, kept_v

        kept = jnp.zeros((16, 128), f32)
        kept_p, kept_v = lax.fori_loop(0, levels // 32, gather, (kept, kept))
        edges[16 * half : 16 * half + 16, :] = kept_p
        edges[32 + 16 * half : 48 + 16 * half, :] = kept_v
    own = jnp.where(block == 0, own_metric[...], 0.0)
    for shift in (4, 8, 16, 32, 64):
        own = own + pltpu.roll(own, shift, 1)
    edges[64:80, :] = own

    def step(k, carry):
        g, before = carry
        here = first + sign * k
        weight = weights[here]
        after = pair[link + sign * k]
        total = weight + before * g
        inverse = 1.0 / (total + after)
        part_a[here] = weight * inverse
        part_b[here] = before * inverse
        part_c[here] = after * inverse
        return total * inverse, after

    zeros = jnp.zeros((4, 16, 128), f32)
    carry = (zeros, zeros)
    for j in range(4):
        if j == 0:
            for copy in copies[0] + copies[1]:
                copy.wait()
        elif j < 3:
            for copy in copies[j + 1]:
                copy.wait()
        count = chunk if j < 3 else chunk - 1
        start = j * chunk
        if count % 8 == 0:
            carry = loop(count, lambda k, c: step(start + k, c), carry, 8)
        else:
            carry = loop(count, lambda k, c: step(start + k, c), carry, 5)
    g, before = carry
    here = first + sign * (levels - 1)
    weight = weights[here]
    inverse = 1.0 / (weight + before * g)
    part_a[here] = weight * inverse
    part_b[here] = before * inverse
    part_c[here] = inverse
    outward = jnp.where(top == 0, 1.0 / pair[levels - 1], zeros)
    resist[...] = inverse + outward
    for copy in late:
        copy.wait()


def pack_y(edges, low_halo, high_halo, out):
    levels = (low_halo.shape[0] - 8) // 3
    block = block_of(8)
    row = row_ids(8)
    kept = jnp.zeros((8, 128), f32)
    for half in range(2):

        def gather(i, kept):
            moved = []
            for j in range(32):
                at = 32 * i + j
                level = half * (levels // 2) + at
                low = jnp.broadcast_to(low_halo[pl.ds(level, 1), :], (8, 128))
                high = jnp.broadcast_to(high_halo[pl.ds(level, 1), :], (8, 128))
                both = pltpu.roll(jnp.where(row == 2 * half, low, high), 4 * at, 1)
                moved.append(((block == at) & (row // 2 == half), both))
            for mine, both in moved:
                kept = jnp.where(mine, both, kept)
            return kept

        kept = lax.fori_loop(0, levels // 64, gather, kept)
    out[0:80, :] = edges[...]
    out[80:88, :] = kept


def interior(fields, low_halo, high_halo, metric, part_a, part_b, partial, done):
    levels = fields.shape[0]
    top, sign, first, link = order(levels)
    row = row_ids(16)
    m = metric[...]
    slope = step_dt * 0.5 * m
    spread = 0.5 * step_dt * sound_sq * m * m
    slope_low = step_dt * 0.5 * low_halo[3 * levels : 3 * levels + 1, :]
    slope_high = step_dt * 0.5 * high_halo[3 * levels : 3 * levels + 1, :]
    batch = 8

    def east(z):
        return pltpu.roll(z, 127, 1)

    def west(z):
        return pltpu.roll(z, 1, 1)

    def below(z, edge):
        return jnp.where(row == 0, edge, pltpu.roll(z, 1, 0))

    def above(z, edge):
        return jnp.where(row == 15, edge, pltpu.roll(z, 15, 0))

    def several(i, carry):
        d_u, d_w = carry
        ls = [first + sign * (i * batch + j) for j in range(batch)]
        pieces = []
        for l in ls:
            p = fields[l, 3]
            u = fields[l, 0]
            v = fields[l, 1]
            near_low = low_halo[pl.ds(l, 1), :]
            far_low = low_halo[pl.ds(levels + l, 1), :]
            u_low = low_halo[pl.ds(2 * levels + l, 1), :]
            near_high = high_halo[pl.ds(l, 1), :]
            far_high = high_halo[pl.ds(levels + l, 1), :]
            u_high = high_halo[pl.ds(2 * levels + l, 1), :]
            drive = fields[l, 2] * part_a[l, 2]
            pieces.append(
                (p, u, v, near_low, far_low, u_low, near_high, far_high, u_high, part_a[l, 0], part_b[l, 0], drive, part_b[l, 2])
            )
        results = []
        for p, u, v, near_low, far_low, u_low, near_high, far_high, u_high, a_u, b_u, drive, b_w in pieces:
            before = below(p, near_low)
            after = above(p, near_high)
            sides = before + after
            outer = below(before, far_low) + above(after, far_high)
            p_east, p_west = east(p), west(p)
            u1 = u - slope * (after - before)
            v1 = v - slope * (p_east - p_west)
            u1_low = u_low - slope_low * (p[0:1] - far_low)
            u1_high = u_high - slope_high * (far_high - p[15:16])
            diff_u = above(u1, u1_high) - below(u1, u1_low)
            diff_v = east(v1) - west(v1)
            inner = (p_east + p_west) + 2.0 * sides - 8.0 * p
            second = outer + (east(inner) + west(inner)) - 8.0 * sides + 18.0 * p
            p1 = p - spread * (diff_u + diff_v) - hyper_nu * second
            results.append((v1, p1, a_u * u1, b_u, drive, b_w))
        for l, (v1, p1, drive_u, b_u, drive_w, b_w) in zip(ls, results):
            partial[l, 0] = v1
            partial[l, 1] = p1
            d_u = drive_u + b_u * d_u
            d_w = drive_w + b_w * d_w
            done[l, 0] = d_u
            done[l, 1] = d_w
        return d_u, d_w

    zeros = jnp.zeros((16, 128), f32)
    lax.fori_loop(0, levels // batch, several, (zeros, zeros))


def finish_forward(partial, done, part_a, part_b, edges, left, right, resist, solved, out, fix_v, fix_p):
    turn = lax.axis_index("gy")
    left = jnp.where(turn == 0, 0.0, left[...])
    right = jnp.where(turn == lax.axis_size("gy") - 1, 0.0, right[...])
    edges = edges[...]
    levels = partial.shape[0]
    top, sign, first, link = order(levels)
    lane = lane_ids(16)
    row = row_ids(16)
    place = lax.rem(lane + 2, 4)
    m = edges[64:80, :]
    slope = step_dt * 0.5 * m
    spread = 0.5 * step_dt * sound_sq * m * m
    slope_left = step_dt * 0.5 * left[64:80, :]
    slope_right = step_dt * 0.5 * right[64:80, :]

    def shift(z, by):
        return pltpu.roll(z, by % 128, 1)

    for half in range(2):
        at = 16 * half

        def sides_of(side):
            p = side[at : at + 16, :] - edges[at : at + 16, :]
            ends = 80 + 2 * half
            low = side[ends : ends + 1, :] - edges[ends : ends + 1, :]
            high = side[ends + 1 : ends + 2, :] - edges[ends + 1 : ends + 2, :]
            before = jnp.where(row == 0, low, pltpu.roll(p, 1, 0))
            after = jnp.where(row == 15, high, pltpu.roll(p, 15, 0))
            return p, 2.0 * (before + after) - 8.0 * p

        p_own = edges[at : at + 16, :]
        p_left, cross_left = sides_of(left)
        p_right, cross_right = sides_of(right)
        p_east, p_west = shift(p_own, -1), shift(p_own, 1)
        v1_own = edges[32 + at : 48 + at, :] - slope * (p_east - p_west)
        v1_left = left[32 + at : 48 + at, :] - slope_left * (p_east - shift(left[at : at + 16, :], 1))
        v1_right = right[32 + at : 48 + at, :] - slope_right * (shift(right[at : at + 16, :], -1) - p_west)
        second = (
            jnp.where(place >= 2, shift(p_left, 2), shift(p_right, -2))
            + jnp.where(place == 2, shift(cross_left, 1), 0.0)
            + jnp.where(place == 1, shift(cross_right, -1), 0.0)
        )
        own_v = jnp.where(
            place == 2, slope * shift(p_left, 1), jnp.where(place == 1, -slope * shift(p_right, -1), 0.0)
        )
        diff_v = jnp.where(
            place == 2,
            shift(v1_own - v1_left, 1),
            jnp.where(
                place == 3,
                -shift(own_v, 1),
                jnp.where(place == 1, shift(v1_right - v1_own, -1), shift(own_v, -1)),
            ),
        )
        fix_v[half] = own_v
        fix_p[half] = -spread * diff_v - hyper_nu * second

    edge = (lane >= 126) | (lane < 2)
    batch = 16

    def segment(turn, carry):
        half = top + sign * turn
        all_v = fix_v[half]
        all_p = fix_p[half]

        def several(i, carry):
            d_v, d_p = carry
            ls = [first + sign * (turn * (levels // 2) + i * batch + j) for j in range(batch)]
            drives = []
            for l in ls:
                back = lax.rem(128 - 4 * (l - half * (levels // 2)), 128)
                v1 = partial[l, 0] + jnp.where(edge, pltpu.roll(all_v, back, 1), 0.0)
                p1 = partial[l, 1] + jnp.where(edge, pltpu.roll(all_p, back, 1), 0.0)
                drives.append((part_a[l, 1] * v1, part_b[l, 1], part_a[l, 3] * p1, part_b[l, 3]))
            for l, (drive_v, b_v, drive_p, b_p) in zip(ls, drives):
                d_v = drive_v + b_v * d_v
                d_p = drive_p + b_p * d_p
                solved[l, 0] = d_v
                solved[l, 1] = d_p
            return d_v, d_p

        return lax.fori_loop(0, levels // (2 * batch), several, carry)

    zeros = jnp.zeros((16, 128), f32)
    d_v, d_p = segment(1, segment(0, (zeros, zeros)))
    last = first + sign * (levels - 1)
    out[0, 0] = done[last, 0]
    out[0, 1] = d_v
    out[0, 2] = done[last, 1]
    out[0, 3] = d_p
    out[1] = resist[...]


def back_substitute(done, solved, part_c, mine, other, out, x_ref, sems):
    levels = done.shape[0]
    top, sign, first, link = order(levels)
    last = first + sign * (levels - 1)
    x = mine[0] + (other[0] - mine[0]) * (part_c[last] / (mine[1] + other[1]))
    x_ref[last] = x
    chunk = levels // 8
    copies = []

    def several(ks, x):
        ls = [last - sign * k for k in ks]
        loaded = [
            (part_c[l], [done[l, 0], solved[l, 0], done[l, 1], solved[l, 1]]) for l in ls
        ]
        for l, (c, d) in zip(ls, loaded):
            x = jnp.stack(d) + c * x
            x_ref[l] = x
        return x

    for j in range(8):
        ks = list(range(j * chunk + (j == 0), (j + 1) * chunk))
        for i in range(0, len(ks), 2):
            x = several(ks[i : i + 2], x)
        at = pl.ds((1 - top) * (levels - chunk) - sign * (j * chunk), chunk)
        copy = pltpu.make_async_copy(x_ref.at[at], out.at[at], sems.at[j])
        copy.start()
        copies.append(copy)
    for copy in copies:
        copy.wait()


def near(shape):
    return pltpu.VMEM(shape, f32)


def plain(shape):
    return jax.ShapeDtypeStruct(shape, f32)


def call(body, ins, outs, scratch=(), cost=0, name=None, aliases=None):
    def run(*args):
        return pl.pallas_call(
            body,
            in_specs=ins,
            out_specs=[VM] * len(outs),
            out_shape=outs,
            scratch_shapes=list(scratch),
            name=name,
            input_output_aliases=aliases or {},
            cost_estimate=pl.CostEstimate(flops=cost, bytes_accessed=cost, transcendentals=0) if cost else None,
            compiler_params=pltpu.CompilerParams(vmem_limit_bytes=LIMIT),
        )(*args)

    return run


def far(x):
    return pltpu.with_memory_space_constraint(x, pltpu.HBM)


def shards(state, metric, couple, base):
    levels = state.shape[0]
    nx, ny = lax.axis_size("gx"), lax.axis_size("gy")
    dma = pltpu.SemaphoreType.DMA
    side = (3 * levels + 8, 128)
    full = (levels, 4, 16, 128)
    two = (levels, 2, 16, 128)
    state, metric, couple, base = far(state), far(metric), far(couple), far(base)

    low_side, high_side = call(
        pack_x, [HB, HB], [plain(side), plain(side)], [dma((8,))], name="pack_x"
    )(state, metric)
    low_halo = lax.ppermute(high_side, "gx", [(i, (i + 1) % nx) for i in range(nx)])
    high_halo = lax.ppermute(low_side, "gx", [((i + 1) % nx, i) for i in range(nx)])

    fields, own_metric, part_a, part_b, part_c, edges, resist = call(
        factor,
        [HB, HB, HB, HB],
        [near(full), near((16, 128)), near(full), near(full), near(full), near((80, 128)), near((4, 16, 128))],
        [pltpu.VMEM(full, f32), pltpu.VMEM(full, f32), dma((13,))],
        cost=8 * 1024 * 1024,
        name="factor",
    )(state, couple, base, metric)

    packed = call(pack_y, [VM] * 3, [plain((88, 128))], name="pack_y")(edges, low_halo, high_halo)[0]
    left = lax.ppermute(packed, "gy", [(i, (i + 1) % ny) for i in range(ny)])
    right = lax.ppermute(packed, "gy", [((i + 1) % ny, i) for i in range(ny)])

    partial, done = call(
        interior,
        [VM] * 6,
        [near(two), near(two)],
        cost=8 * 1024 * 1024,
        name="interior",
    )(fields, low_halo, high_halo, own_metric, part_a, part_b)

    solved, mine = call(
        finish_forward,
        [VM] * 8,
        [near(two), plain((2, 4, 16, 128))],
        [pltpu.VMEM((2, 16, 128), f32), pltpu.VMEM((2, 16, 128), f32)],
        name="finish_forward",
    )(partial, done, part_a, part_b, packed, left, right, resist)
    other = lax.ppermute(mine, "gz", [(0, 1), (1, 0)])

    return pl.pallas_call(
        back_substitute,
        in_specs=[VM] * 5,
        out_specs=pl.BlockSpec(memory_space=pl.ANY),
        out_shape=plain(full),
        scratch_shapes=[pltpu.VMEM(full, f32), dma((8,))],
        name="back_substitute",
        compiler_params=pltpu.CompilerParams(vmem_limit_bytes=LIMIT),
    )(done, solved, part_c, mine, other)


def solution(mesh):
    in_specs = (
        P("gz", None, "gx", "gy"),
        P("gx", "gy"),
        P("gz", None, "gx", "gy"),
        P("gz", None, "gx", "gy"),
    )
    out_specs = P("gz", None, "gx", "gy")
    return jax.shard_map(shards, mesh=mesh, in_specs=in_specs, out_specs=out_specs, check_vma=False)
```

time: 33.7 us -> 26 us (0.77)
  the two profiles are of different devices: /device:TPU:1 before, /device:TPU:16 now
where the time goes in v2:
time: 26 us; the launch traced here: 25.8 us
  starting transfers between devices  9.38 us (36%)
  Pallas kernels  8.32 us (32%)
  waiting for transfers between devices  8.05 us (31%)
    pallas_call x5, Pallas kernels, run(): pl.pallas_call(body, in_specs=ins, out_specs=[VM] * len(outs), out_shape=...  6.76 us
    ppermute x1, starting transfers between devices, shards(): lax.ppermute(low_side, 'gx', [((i + 1) % nx, i) for i in range(nx)])  5.38 us
    ppermute x1, waiting for transfers between devices, shards(): other = lax.ppermute(mine, 'gz', [(0, 1), (1, 0)])  5.14 us
    ppermute x1, waiting for transfers between devices, shards(): left = lax.ppermute(packed, 'gy', [(i, (i + 1) % ny) for i in range(ny)])  2.9 us
    ppermute x1, starting transfers between devices, shards(): right = lax.ppermute(packed, 'gy', [((i + 1) % ny, i) for i in range(ny)])  1.93 us
    pallas_call x1, Pallas kernels, shards(): pl.pallas_call(back_substitute, in_specs=[VM] * 5, out_specs=pl.BlockSpec...  1.56 us
    ppermute x1, starting transfers between devices, shards(): lax.ppermute(high_side, 'gx', [(i, (i + 1) % nx) for i in range(nx)])  1.36 us
    ppermute x1, starting transfers between devices, shards(): other = lax.ppermute(mine, 'gz', [(0, 1), (1, 0)])  0.71 us
  transfers between devices with their start and end apart: 5, of which 2 were waited for; matrix products, arithmetic and copies ran while one was open for 0% of the time, Pallas kernels for 19%

profile of v2, /device:TPU:16, one launch (start us, length us, event | category | flops | bytes accessed | tf_op | source)
XLA Modules:
  0.0 25.8 jit_solution(10757229169978550559)
XLA Ops:
  0.0 0.9 %pack_x.1 = (f32[200,128]{1,0:T(8,128)S(1)}, f32[200,128]{1,0:T(8,128)S(1)}) custom-call(f32[64,4,16,128]{3,2,1,0:T(8,128)} %state.3, f32[16,128]{1,0:T(8,128)} %metric.3), custom_call_target="tpu_custom_call" | custom-call | tf_op jit(solution)/shard_map/pack_x/pallas_call | solution.py:385
  1.0 1.4 %collective-permute-start = (f32[200,128]{1,0:T(8,128)S(1)}, f32[200,128]{1,0:T(8,128)S(1)}, u32[]{:S(2)}, u32[]{:S(2)}) collective-permute-start(f32[200,128]{1,0:T(8,128)S(1)} %get-tuple-element.19), channel_id=1, source_target_pairs={{0,16},{16,32},{32,48},{48,64},{64,80},{80,96},{96,112},{112,128},... | collective-permute-start | bytes 307208 | tf_op jit(solution)/shard_map/ppermute | solution.py:416
  2.3 5.4 %collective-permute-start.1 = (f32[200,128]{1,0:T(8,128)S(1)}, f32[200,128]{1,0:T(8,128)S(1)}, u32[]{:S(2)}, u32[]{:S(2)}) collective-permute-start(f32[200,128]{1,0:T(8,128)S(1)} %get-tuple-element.20), channel_id=1, source_target_pairs={{16,0},{32,16},{48,32},{64,48},{80,64},{96,80},{112,96},{128,112},... | collective-permute-start | bytes 307208 | tf_op jit(solution)/shard_map/ppermute | solution.py:417
  7.7 3.2 %factor.1 = (f32[64,4,16,128]{3,2,1,0:T(8,128)S(1)}, f32[16,128]{1,0:T(8,128)S(1)}, f32[64,4,16,128]{3,2,1,0:T(8,128)S(1)}, f32[64,4,16,128]{3,2,1,0:T(8,128)S(1...) custom-call(f32[64,4,16,128]{3,2,1,0:T(8,128)} %state.3, ...), custom_call_target="tpu_custom_call" | custom-call | flops 8388608 | bytes 8388608 | tf_op jit(solution)/shard_map/factor/pallas_call | solution.py:385
  10.9 0.0 collective-permute-done.low_halo
  10.9 0.0 collective-permute-done.1.high_halo
  10.9 0.1 pack_y.1.edges
  11.0 1.9 %collective-permute-start.3 = (f32[88,128]{1,0:T(8,128)S(1)}, f32[88,128]{1,0:T(8,128)S(1)}, u32[]{:S(2)}, u32[]{:S(2)}) collective-permute-start(f32[88,128]{1,0:T(8,128)S(1)} %pack_y.1.edges), channel_id=1, source_target_pairs={{2,0},{4,2},{6,4},{8,6},{10,8},{12,10},{14,12},{0,14},{3,1},{5,3},... | collective-permute-start | bytes 135176 | tf_op jit(solution)/shard_map/ppermute | solution.py:430
  13.0 0.0 collective-permute-start.2
  13.0 1.8 %interior.1 = (f32[64,2,16,128]{3,2,1,0:T(8,128)S(1)}, f32[64,2,16,128]{3,2,1,0:T(8,128)S(1)}) custom-call(f32[64,4,16,128]{3,2,1,0:T(8,128)S(1)} %get-tuple-element.18.fields, f32[200,128]{1,0:T(8,128)S(1)} %collective-permute-done.low_halo, f32[200,128]{1,0:T(8,128)S(1)} %collective-permute-done.1.high_halo, f32[16,128]{1,0:T(8,128)S(1)} %get-tuple-element.21.metric, ...), custom_call_target="tpu_custom_call" | custom-call | flops 8388608 | bytes 8388608 | tf_op jit(solution)/shard_map/interior/pallas_call | solution.py:385
  14.7 0.0 collective-permute-done.3.right
  14.8 2.9 %collective-permute-done.2.left = f32[88,128]{1,0:T(8,128)S(1)} collective-permute-done((f32[88,128]{1,0:T(8,128)S(1)}, f32[88,128]{1,0:T(8,128)S(1)}, u32[]{:S(2)}, u32[]{:S(2)}) %collective-permute-start.2) | collective-permute-done | bytes 45088 | tf_op jit(solution)/shard_map/ppermute | solution.py:429
  17.7 0.7 %finish_forward.1 = (f32[64,2,16,128]{3,2,1,0:T(8,128)S(1)}, f32[2,4,16,128]{3,2,1,0:T(8,128)S(1)}) custom-call(f32[64,2,16,128]{3,2,1,0:T(8,128)S(1)} %get-tuple-element.25.partial, f32[64,2,16,128]{3,2,1,0:T(8,128)S(1)} %get-tuple-element.24.done, f32[64,4,16,128]{3,2,1,0:T(8,128)S(1)} %get-tuple-element.22.part_a, ...), custom_call_target="tpu_custom_call" | custom-call | tf_op jit(solution)/shard_map/finish_forward/pallas_call | solution.py:385
  18.4 0.7 %collective-permute-start.4 = (f32[2,4,16,128]{3,2,1,0:T(8,128)S(1)}, f32[2,4,16,128]{3,2,1,0:T(8,128)S(1)}, u32[]{:S(2)}, u32[]{:S(2)}) collective-permute-start(f32[2,4,16,128]{3,2,1,0:T(8,128)S(1)} %get-tuple-element.30.mine), channel_id=1, source_target_pairs={{0,1},{1,0},{2,3},{3,2},{4,5},{5,4},{6,7},{7,6},{8,9},{9,8},{10,11... | collective-permute-start | bytes 196616 | tf_op jit(solution)/shard_map/ppermute | solution.py:447
  19.1 5.1 %collective-permute-done.4.other = f32[2,4,16,128]{3,2,1,0:T(8,128)S(1)} collective-permute-done((f32[2,4,16,128]{3,2,1,0:T(8,128)S(1)}, f32[2,4,16,128]{3,2,1,0:T(8,128)S(1)}, u32[]{:S(2)}, u32[]{:S(2)}) %collective-permute-start.4) | collective-permute-done | bytes 65568 | tf_op jit(solution)/shard_map/ppermute | solution.py:447
  24.3 1.6 %back_substitute.1 = f32[64,4,16,128]{3,2,1,0:T(8,128)} custom-call(f32[64,2,16,128]{3,2,1,0:T(8,128)S(1)} %get-tuple-element.24.done, f32[64,2,16,128]{3,2,1,0:T(8,128)S(1)} %get-tuple-element.28.solved, f32[64,4,16,128]{3,2,1,0:T(8,128)S(1)} %get-tuple-element.29.part_c, f32[2,4,16,128]{3,2,1,0:T(8,128)S(1)} %get-tuple-element.30.mine, ...), custom_call_target="tpu_custom_call" | custom-call | tf_op jit(solution)/shard_map/back_substitute/pallas_call | solution.py:449
Async XLA Ops:
  1.0 9.9 %collective-permute-start = (f32[200,128]{1,0:T(8,128)S(1)}, f32[200,128]{1,0:T(8,128)S(1)}, u32[]{:S(2)}, u32[]{:S(2)}) collective-permute-start(f32[200,128]{1,0:T(8,128)S(1)} %get-tuple-element.19), channel_id=1, source_target_pairs={{0,16},{16,32},{32,48},{48,64},{64,80},{80,96},{96,112},{112,128},... | collective-permute-start | bytes 307208 | tf_op jit(solution)/shard_map/ppermute | solution.py:416
  2.3 8.6 %collective-permute-start.1 = (f32[200,128]{1,0:T(8,128)S(1)}, f32[200,128]{1,0:T(8,128)S(1)}, u32[]{:S(2)}, u32[]{:S(2)}) collective-permute-start(f32[200,128]{1,0:T(8,128)S(1)} %get-tuple-element.20), channel_id=1, source_target_pairs={{16,0},{32,16},{48,32},{64,48},{80,64},{96,80},{112,96},{128,112},... | collective-permute-start | bytes 307208 | tf_op jit(solution)/shard_map/ppermute | solution.py:417
  11.0 3.7 %collective-permute-start.3 = (f32[88,128]{1,0:T(8,128)S(1)}, f32[88,128]{1,0:T(8,128)S(1)}, u32[]{:S(2)}, u32[]{:S(2)}) collective-permute-start(f32[88,128]{1,0:T(8,128)S(1)} %pack_y.1.edges), channel_id=1, source_target_pairs={{2,0},{4,2},{6,4},{8,6},{10,8},{12,10},{14,12},{0,14},{3,1},{5,3},... | collective-permute-start | bytes 135176 | tf_op jit(solution)/shard_map/ppermute | solution.py:430
  13.0 4.7 %collective-permute-start.2 = (f32[88,128]{1,0:T(8,128)S(1)}, f32[88,128]{1,0:T(8,128)S(1)}, u32[]{:S(2)}, u32[]{:S(2)}) collective-permute-start(f32[88,128]{1,0:T(8,128)S(1)} %pack_y.1.edges), channel_id=1, source_target_pairs={{0,2},{2,4},{4,6},{6,8},{8,10},{10,12},{12,14},{14,0},{1,3},{3,5},... | collective-permute-start | bytes 135176 | tf_op jit(solution)/shard_map/ppermute | solution.py:429
  18.4 5.9 %collective-permute-start.4 = (f32[2,4,16,128]{3,2,1,0:T(8,128)S(1)}, f32[2,4,16,128]{3,2,1,0:T(8,128)S(1)}, u32[]{:S(2)}, u32[]{:S(2)}) collective-permute-start(f32[2,4,16,128]{3,2,1,0:T(8,128)S(1)} %get-tuple-element.30.mine), channel_id=1, source_target_pairs={{0,1},{1,0},{2,3},{3,2},{4,5},{5,4},{6,7},{7,6},{8,9},{9,8},{10,11... | collective-permute-start | bytes 196616 | tf_op jit(solution)/shard_map/ppermute | solution.py:447

commit v3 on v2

--- a/solution.py
+++ b/solution.py
@@ -60,7 +60,7 @@
     return lax.rem(lane_ids(rows) + 2, 128) // 4
 
 
-def factor(state, couple, base, metric, fields, own_metric, part_a, part_b, part_c, edges, resist, pair, weights, sems):
+def factor(state, couple, base, metric, fields, own_metric, part_a, part_b, part_c, edges, sides, resist, pair, weights, sems):
     levels = fields.shape[0]
     top, sign, first, link = order(levels)
     chunk = levels // 4
@@ -110,6 +110,17 @@
     for shift in (4, 8, 16, 32, 64):
         own = own + pltpu.roll(own, shift, 1)
     edges[64:80, :] = own
+    place = lax.rem(lane_ids(16) + 2, 4)
+    for half in range(2):
+        at = 16 * half
+        p = edges[at : at + 16, :]
+        v = edges[32 + at : 48 + at, :]
+        sides[0, at : at + 16, :] = jnp.where(
+            place < 2, p, jnp.where(place == 2, pltpu.roll(v, 1, 1), pltpu.roll(own, 2, 1))
+        )
+        sides[1, at : at + 16, :] = jnp.where(
+            place >= 2, p, jnp.where(place == 1, pltpu.roll(v, 127, 1), pltpu.roll(own, 126, 1))
+        )
 
     def step(k, carry):
         g, before = carry
@@ -151,7 +162,7 @@
         copy.wait()
 
 
-def pack_y(edges, low_halo, high_halo, out):
+def pack_y(sides, low_halo, high_halo, on_chip, off_chip, ends):
     levels = (low_halo.shape[0] - 8) // 3
     block = block_of(8)
     row = row_ids(8)
@@ -172,11 +183,14 @@
             return kept
 
         kept = lax.fori_loop(0, levels // 64, gather, kept)
-    out[0:80, :] = edges[...]
-    out[80:88, :] = kept
-
-
-def interior(fields, low_halo, high_halo, metric, part_a, part_b, partial, done):
+    odd = lax.rem(lax.axis_index("gy"), 2)
+    for out, side in ((on_chip, odd), (off_chip, 1 - odd)):
+        out[0:32, :] = sides[side]
+        out[32:40, :] = kept
+    ends[...] = kept
+
+
+def interior(fields, low_halo, high_halo, metric, part_a, part_b, done, reach):
     levels = fields.shape[0]
     top, sign, first, link = order(levels)
     row = row_ids(16)
@@ -199,26 +213,28 @@
     def above(z, edge):
         return jnp.where(row == 15, edge, pltpu.roll(z, 15, 0))
 
-    def several(i, carry):
-        d_u, d_w = carry
+    def several(i, d):
         ls = [first + sign * (i * batch + j) for j in range(batch)]
         pieces = []
         for l in ls:
-            p = fields[l, 3]
-            u = fields[l, 0]
-            v = fields[l, 1]
-            near_low = low_halo[pl.ds(l, 1), :]
-            far_low = low_halo[pl.ds(levels + l, 1), :]
-            u_low = low_halo[pl.ds(2 * levels + l, 1), :]
-            near_high = high_halo[pl.ds(l, 1), :]
-            far_high = high_halo[pl.ds(levels + l, 1), :]
-            u_high = high_halo[pl.ds(2 * levels + l, 1), :]
-            drive = fields[l, 2] * part_a[l, 2]
             pieces.append(
-                (p, u, v, near_low, far_low, u_low, near_high, far_high, u_high, part_a[l, 0], part_b[l, 0], drive, part_b[l, 2])
+                (
+                    fields[l, 3],
+                    fields[l, 0],
+                    fields[l, 1],
+                    low_halo[pl.ds(l, 1), :],
+                    low_halo[pl.ds(levels + l, 1), :],
+                    low_halo[pl.ds(2 * levels + l, 1), :],
+                    high_halo[pl.ds(l, 1), :],
+                    high_halo[pl.ds(levels + l, 1), :],
+                    high_halo[pl.ds(2 * levels + l, 1), :],
+                    [part_a[l, f] for f in range(4)],
+                    [part_b[l, f] for f in range(4)],
+                    fields[l, 2],
+                )
             )
         results = []
-        for p, u, v, near_low, far_low, u_low, near_high, far_high, u_high, a_u, b_u, drive, b_w in pieces:
+        for p, u, v, near_low, far_low, u_low, near_high, far_high, u_high, a, b, w in pieces:
             before = below(p, near_low)
             after = above(p, near_high)
             sides = before + after
@@ -233,35 +249,62 @@
             inner = (p_east + p_west) + 2.0 * sides - 8.0 * p
             second = outer + (east(inner) + west(inner)) - 8.0 * sides + 18.0 * p
             p1 = p - spread * (diff_u + diff_v) - hyper_nu * second
-            results.append((v1, p1, a_u * u1, b_u, drive, b_w))
-        for l, (v1, p1, drive_u, b_u, drive_w, b_w) in zip(ls, results):
-            partial[l, 0] = v1
-            partial[l, 1] = p1
-            d_u = drive_u + b_u * d_u
-            d_w = drive_w + b_w * d_w
-            done[l, 0] = d_u
-            done[l, 1] = d_w
-        return d_u, d_w
+            results.append(([a[f] * z for f, z in enumerate((u1, v1, w, p1))], b))
+        for l, (drive, b) in zip(ls, results):
+            d = tuple(drive[f] + b[f] * d[f] for f in range(4))
+            for f in range(4):
+                done[l, f] = d[f]
+        return d
 
     zeros = jnp.zeros((16, 128), f32)
-    lax.fori_loop(0, levels // batch, several, (zeros, zeros))
-
-
-def finish_forward(partial, done, part_a, part_b, edges, left, right, resist, solved, out, fix_v, fix_p):
+    lax.fori_loop(0, levels // batch, several, (zeros,) * 4)
+
+    block = block_of(16)
+
+    reach_batch = 32
+
+    def segment(half, onward):
+        def gather(i, carry):
+            (on_v, on_p), (kept_v, kept_p) = carry
+            moved = []
+            for j in range(reach_batch):
+                k = levels - 1 - ((1 - half) * (levels // 2) + i * reach_batch + j)
+                l = first + sign * k
+                at = lax.rem(l, levels // 2)
+                moved.append(
+                    (block == at, pltpu.roll(part_a[l, 1] * on_v, 4 * at, 1), pltpu.roll(part_a[l, 3] * on_p, 4 * at, 1))
+                )
+                on_v = part_b[l, 1] * on_v
+                on_p = part_b[l, 3] * on_p
+            for mine, v, p in moved:
+                kept_v = jnp.where(mine, v, kept_v)
+                kept_p = jnp.where(mine, p, kept_p)
+            return (on_v, on_p), (kept_v, kept_p)
+
+        onward, kept = lax.fori_loop(0, levels // (2 * reach_batch), gather, (onward, (zeros, zeros)))
+        at = half + top * (1 - 2 * half)
+        reach[0, at] = kept[0]
+        reach[1, at] = kept[1]
+        return onward
+
+    ones = jnp.ones((16, 128), f32)
+    segment(0, segment(1, (ones, ones)))
+
+
+def finish_forward(done, edges, ends, on_chip, off_chip, reach, resist, out, fixes):
+    levels = done.shape[0]
+    top, sign, first, link = order(levels)
     turn = lax.axis_index("gy")
-    left = jnp.where(turn == 0, 0.0, left[...])
-    right = jnp.where(turn == lax.axis_size("gy") - 1, 0.0, right[...])
-    edges = edges[...]
-    levels = partial.shape[0]
-    top, sign, first, link = order(levels)
+    odd = lax.rem(turn, 2) == 1
+    near_side, far_side = on_chip[...], off_chip[...]
+    left = jnp.where(turn == 0, 0.0, jnp.where(odd, near_side, far_side))
+    right = jnp.where(turn == lax.axis_size("gy") - 1, 0.0, jnp.where(odd, far_side, near_side))
     lane = lane_ids(16)
     row = row_ids(16)
     place = lax.rem(lane + 2, 4)
     m = edges[64:80, :]
     slope = step_dt * 0.5 * m
     spread = 0.5 * step_dt * sound_sq * m * m
-    slope_left = step_dt * 0.5 * left[64:80, :]
-    slope_right = step_dt * 0.5 * right[64:80, :]
 
     def shift(z, by):
         return pltpu.roll(z, by % 128, 1)
@@ -271,9 +314,8 @@
 
         def sides_of(side):
             p = side[at : at + 16, :] - edges[at : at + 16, :]
-            ends = 80 + 2 * half
-            low = side[ends : ends + 1, :] - edges[ends : ends + 1, :]
-            high = side[ends + 1 : ends + 2, :] - edges[ends + 1 : ends + 2, :]
+            low = side[32 + 2 * half : 33 + 2 * half, :] - ends[2 * half : 2 * half + 1, :]
+            high = side[33 + 2 * half : 34 + 2 * half, :] - ends[2 * half + 1 : 2 * half + 2, :]
             before = jnp.where(row == 0, low, pltpu.roll(p, 1, 0))
             after = jnp.where(row == 15, high, pltpu.roll(p, 15, 0))
             return p, 2.0 * (before + after) - 8.0 * p
@@ -283,8 +325,11 @@
         p_right, cross_right = sides_of(right)
         p_east, p_west = shift(p_own, -1), shift(p_own, 1)
         v1_own = edges[32 + at : 48 + at, :] - slope * (p_east - p_west)
-        v1_left = left[32 + at : 48 + at, :] - slope_left * (p_east - shift(left[at : at + 16, :], 1))
-        v1_right = right[32 + at : 48 + at, :] - slope_right * (shift(right[at : at + 16, :], -1) - p_west)
+        from_left, from_right = left[at : at + 16, :], right[at : at + 16, :]
+        slope_left = step_dt * 0.5 * shift(from_left, -2)
+        slope_right = step_dt * 0.5 * shift(from_right, 2)
+        v1_left = shift(from_left, -1) - slope_left * (p_east - shift(from_left, 1))
+        v1_right = shift(from_right, 1) - slope_right * (shift(from_right, -1) - p_west)
         second = (
             jnp.where(place >= 2, shift(p_left, 2), shift(p_right, -2))
             + jnp.where(place == 2, shift(cross_left, 1), 0.0)
@@ -302,46 +347,61 @@
                 jnp.where(place == 1, shift(v1_right - v1_own, -1), shift(own_v, -1)),
             ),
         )
-        fix_v[half] = own_v
-        fix_p[half] = -spread * diff_v - hyper_nu * second
-
+        fix_p = -spread * diff_v - hyper_nu * second
+        fixes[0, half] = own_v
+        fixes[1, half] = fix_p
+        sum_v = reach[0, half] * own_v + (sum_v if half else 0.0)
+        sum_p = reach[1, half] * fix_p + (sum_p if half else 0.0)
+
+    for by in (4, 8, 16, 32, 64):
+        sum_v = sum_v + shift(sum_v, by)
+        sum_p = sum_p + shift(sum_p, by)
+    edge = (lane >= 126) | (lane < 2)
+    last = done[first + sign * (levels - 1)]
+    out[0, 0] = last[0]
+    out[0, 1] = last[1] + jnp.where(edge, sum_v, 0.0)
+    out[0, 2] = last[2]
+    out[0, 3] = last[3] + jnp.where(edge, sum_p, 0.0)
+    out[1] = resist[...]
+
+
+def settle(before, part_a, part_b, fixes, done):
+    levels = before.shape[0]
+    top, sign, first, link = order(levels)
+    lane = lane_ids(16)
     edge = (lane >= 126) | (lane < 2)
     batch = 16
 
     def segment(turn, carry):
         half = top + sign * turn
-        all_v = fix_v[half]
-        all_p = fix_p[half]
+        all_v = fixes[0, half]
+        all_p = fixes[1, half]
 
         def several(i, carry):
-            d_v, d_p = carry
+            e_v, e_p = carry
             ls = [first + sign * (turn * (levels // 2) + i * batch + j) for j in range(batch)]
             drives = []
             for l in ls:
                 back = lax.rem(128 - 4 * (l - half * (levels // 2)), 128)
-                v1 = partial[l, 0] + jnp.where(edge, pltpu.roll(all_v, back, 1), 0.0)
-                p1 = partial[l, 1] + jnp.where(edge, pltpu.roll(all_p, back, 1), 0.0)
-                drives.append((part_a[l, 1] * v1, part_b[l, 1], part_a[l, 3] * p1, part_b[l, 3]))
-            for l, (drive_v, b_v, drive_p, b_p) in zip(ls, drives):
-                d_v = drive_v + b_v * d_v
-                d_p = drive_p + b_p * d_p
-                solved[l, 0] = d_v
-                solved[l, 1] = d_p
-            return d_v, d_p
+                v1 = jnp.where(edge, pltpu.roll(all_v, back, 1), 0.0)
+                p1 = jnp.where(edge, pltpu.roll(all_p, back, 1), 0.0)
+                drives.append(
+                    (part_a[l, 1] * v1, part_b[l, 1], part_a[l, 3] * p1, part_b[l, 3], before[l, 1], before[l, 3])
+                )
+            for l, (drive_v, b_v, drive_p, b_p, d_v, d_p) in zip(ls, drives):
+                e_v = drive_v + b_v * e_v
+                e_p = drive_p + b_p * e_p
+                done[l, 1] = d_v + e_v
+                done[l, 3] = d_p + e_p
+            return e_v, e_p
 
         return lax.fori_loop(0, levels // (2 * batch), several, carry)
 
     zeros = jnp.zeros((16, 128), f32)
-    d_v, d_p = segment(1, segment(0, (zeros, zeros)))
-    last = first + sign * (levels - 1)
-    out[0, 0] = done[last, 0]
-    out[0, 1] = d_v
-    out[0, 2] = done[last, 1]
-    out[0, 3] = d_p
-    out[1] = resist[...]
-
-
-def back_substitute(done, solved, part_c, mine, other, out, x_ref, sems):
+    segment(1, segment(0, (zeros, zeros)))
+
+
+def back_substitute(done, part_c, mine, other, out, x_ref, sems):
     levels = done.shape[0]
     top, sign, first, link = order(levels)
     last = first + sign * (levels - 1)
@@ -352,11 +412,9 @@
 
     def several(ks, x):
         ls = [last - sign * k for k in ks]
-        loaded = [
-            (part_c[l], [done[l, 0], solved[l, 0], done[l, 1], solved[l, 1]]) for l in ls
-        ]
+        loaded = [(part_c[l], done[l]) for l in ls]
         for l, (c, d) in zip(ls, loaded):
-            x = jnp.stack(d) + c * x
+            x = d + c * x
             x_ref[l] = x
         return x
 
@@ -407,7 +465,6 @@
     dma = pltpu.SemaphoreType.DMA
     side = (3 * levels + 8, 128)
     full = (levels, 4, 16, 128)
-    two = (levels, 2, 16, 128)
     state, metric, couple, base = far(state), far(metric), far(couple), far(base)
 
     low_side, high_side = call(
@@ -416,45 +473,62 @@
     low_halo = lax.ppermute(high_side, "gx", [(i, (i + 1) % nx) for i in range(nx)])
     high_halo = lax.ppermute(low_side, "gx", [((i + 1) % nx, i) for i in range(nx)])
 
-    fields, own_metric, part_a, part_b, part_c, edges, resist = call(
+    fields, own_metric, part_a, part_b, part_c, edges, sides, resist = call(
         factor,
         [HB, HB, HB, HB],
-        [near(full), near((16, 128)), near(full), near(full), near(full), near((80, 128)), near((4, 16, 128))],
+        [near(full), near((16, 128)), near(full), near(full), near(full), near((80, 128)), near((2, 32, 128)), near((4, 16, 128))],
         [pltpu.VMEM(full, f32), pltpu.VMEM(full, f32), dma((13,))],
         cost=8 * 1024 * 1024,
         name="factor",
     )(state, couple, base, metric)
 
-    packed = call(pack_y, [VM] * 3, [plain((88, 128))], name="pack_y")(edges, low_halo, high_halo)[0]
-    left = lax.ppermute(packed, "gy", [(i, (i + 1) % ny) for i in range(ny)])
-    right = lax.ppermute(packed, "gy", [((i + 1) % ny, i) for i in range(ny)])
-
-    partial, done = call(
+    part = (40, 128)
+    on_chip, off_chip, ends = call(
+        pack_y, [VM] * 3, [plain(part), plain(part), near((8, 128))], name="pack_y"
+    )(sides, low_halo, high_halo)
+    swaps = []
+    for i in range(nx):
+        for j in range(ny):
+            there = (i ^ 1, j) if j in (0, ny - 1) else (i, j + 1 if j % 2 else j - 1)
+            swaps.append((i * ny + j, there[0] * ny + there[1]))
+    off_chip = lax.ppermute(off_chip, ("gx", "gy"), swaps)
+    on_chip = lax.ppermute(on_chip, "gy", [(j, j ^ 1) for j in range(ny)])
+
+    edge = (2, 2, 16, 128)
+    done, reach = call(
         interior,
         [VM] * 6,
-        [near(two), near(two)],
+        [near(full), near(edge)],
         cost=8 * 1024 * 1024,
         name="interior",
     )(fields, low_halo, high_halo, own_metric, part_a, part_b)
 
-    solved, mine = call(
+    mine, fixes = call(
         finish_forward,
-        [VM] * 8,
-        [near(two), plain((2, 4, 16, 128))],
-        [pltpu.VMEM((2, 16, 128), f32), pltpu.VMEM((2, 16, 128), f32)],
+        [VM] * 7,
+        [plain((2, 4, 16, 128)), near(edge)],
         name="finish_forward",
-    )(partial, done, part_a, part_b, packed, left, right, resist)
+    )(done, edges, ends, on_chip, off_chip, reach, resist)
     other = lax.ppermute(mine, "gz", [(0, 1), (1, 0)])
+
+    done = call(
+        settle,
+        [VM] * 4,
+        [near(full)],
+        cost=8 * 1024 * 1024,
+        name="settle",
+        aliases={0: 0},
+    )(done, part_a, part_b, fixes)[0]
 
     return pl.pallas_call(
         back_substitute,
-        in_specs=[VM] * 5,
+        in_specs=[VM] * 4,
         out_specs=pl.BlockSpec(memory_space=pl.ANY),
         out_shape=plain(full),
         scratch_shapes=[pltpu.VMEM(full, f32), dma((8,))],
         name="back_substitute",
         compiler_params=pltpu.CompilerParams(vmem_limit_bytes=LIMIT),
-    )(done, solved, part_c, mine, other)
+    )(done, part_c, mine, other)
 
 
 def solution(mesh):

time: 26 us -> 23.4 us (0.90); the launches traced: 25.8 us -> 22.9 us
  waiting for transfers between devices: 8.05 us -> 6.17 us
  starting transfers between devices: 9.38 us -> 7.56 us
  Pallas kernels: 8.32 us -> 9.11 us
    ppermute x2, starting transfers between devices: 1.93 us -> 0.19 us  [the longest x1 0.09 us: shards(): on_chip = lax.ppermute(on_chip, 'gy', [(j, j ^ 1) for j in range(ny)])]
    ppermute x2, waiting for transfers between devices: 2.9 us -> 1.63 us  [the longest x1 1.63 us: shards(): off_chip = lax.ppermute(off_chip, ('gx', 'gy'), swaps)]
    pallas_call x5 -> x6, Pallas kernels: 6.76 us -> 7.59 us  [run(): pl.pallas_call(body, in_specs=ins, out_specs=[VM] * len(outs), out_shape=...]
    ppermute x1, waiting for transfers between devices: 5.14 us -> 4.53 us  [shards(): other = lax.ppermute(mine, 'gz', [(0, 1), (1, 0)])]
  transfers between devices with their start and end apart: 5 -> 5, of which waited for: 2 -> 2; matrix products, arithmetic and copies ran while one was open for 0% -> 0% of each run, Pallas kernels for 19% -> 26%
where the time goes in v3:
time: 23.4 us; the launch traced here: 22.9 us
  Pallas kernels  9.11 us (39%)
  starting transfers between devices  7.56 us (32%)
  waiting for transfers between devices  6.17 us (26%)
    pallas_call x6, Pallas kernels, run(): pl.pallas_call(body, in_specs=ins, out_specs=[VM] * len(outs), out_shape=...  7.59 us
    ppermute x1, starting transfers between devices, shards(): lax.ppermute(low_side, 'gx', [((i + 1) % nx, i) for i in range(nx)])  5.38 us
    ppermute x1, waiting for transfers between devices, shards(): other = lax.ppermute(mine, 'gz', [(0, 1), (1, 0)])  4.53 us
    ppermute x1, waiting for transfers between devices, shards(): off_chip = lax.ppermute(off_chip, ('gx', 'gy'), swaps)  1.63 us
    pallas_call x1, Pallas kernels, shards(): pl.pallas_call(back_substitute, in_specs=[VM] * 4, out_specs=pl.BlockSpec...  1.52 us
    ppermute x1, starting transfers between devices, shards(): lax.ppermute(high_side, 'gx', [(i, (i + 1) % nx) for i in range(nx)])  1.36 us
    ppermute x1, starting transfers between devices, shards(): other = lax.ppermute(mine, 'gz', [(0, 1), (1, 0)])  0.64 us
  transfers between devices with their start and end apart: 5, of which 2 were waited for; matrix products, arithmetic and copies ran while one was open for 0% of the time, Pallas kernels for 26%

profile of v3, /device:TPU:16, one launch (start us, length us, event | category | flops | bytes accessed | tf_op | source)
XLA Modules:
  0.0 22.9 jit_solution(17223563264049140684)
XLA Ops:
  0.0 0.9 %pack_x.1 = (f32[200,128]{1,0:T(8,128)S(1)}, f32[200,128]{1,0:T(8,128)S(1)}) custom-call(f32[64,4,16,128]{3,2,1,0:T(8,128)} %state.3, f32[16,128]{1,0:T(8,128)} %metric.3), custom_call_target="tpu_custom_call" | custom-call | tf_op jit(solution)/shard_map/pack_x/pallas_call | solution.py:443
  1.0 1.4 %collective-permute-start = (f32[200,128]{1,0:T(8,128)S(1)}, f32[200,128]{1,0:T(8,128)S(1)}, u32[]{:S(2)}, u32[]{:S(2)}) collective-permute-start(f32[200,128]{1,0:T(8,128)S(1)} %get-tuple-element.23), channel_id=1, source_target_pairs={{0,16},{16,32},{32,48},{48,64},{64,80},{80,96},{96,112},{112,128},... | collective-permute-start | bytes 307208 | tf_op jit(solution)/shard_map/ppermute | solution.py:473
  2.3 5.4 %collective-permute-start.1 = (f32[200,128]{1,0:T(8,128)S(1)}, f32[200,128]{1,0:T(8,128)S(1)}, u32[]{:S(2)}, u32[]{:S(2)}) collective-permute-start(f32[200,128]{1,0:T(8,128)S(1)} %get-tuple-element.24), channel_id=1, source_target_pairs={{16,0},{32,16},{48,32},{64,48},{80,64},{96,80},{112,96},{128,112},... | collective-permute-start | bytes 307208 | tf_op jit(solution)/shard_map/ppermute | solution.py:474
  7.7 3.3 %factor.1 = (f32[64,4,16,128]{3,2,1,0:T(8,128)S(1)}, f32[16,128]{1,0:T(8,128)S(1)}, f32[64,4,16,128]{3,2,1,0:T(8,128)S(1)}, f32[64,4,16,128]{3,2,1,0:T(8,128)S(1...) custom-call(f32[64,4,16,128]{3,2,1,0:T(8,128)} %state.3, ...), custom_call_target="tpu_custom_call" | custom-call | flops 8388608 | bytes 8388608 | tf_op jit(solution)/shard_map/factor/pallas_call | solution.py:443
  11.0 0.0 collective-permute-done.low_halo
  11.0 0.0 collective-permute-done.1.high_halo
  11.0 0.1 pack_y.1
  11.1 0.1 collective-permute-start.2
  11.2 0.1 collective-permute-start.3
  11.3 2.1 %interior.1 = (f32[64,4,16,128]{3,2,1,0:T(8,128)S(1)}, f32[2,2,16,128]{3,2,1,0:T(8,128)S(1)}) custom-call(f32[64,4,16,128]{3,2,1,0:T(8,128)S(1)} %get-tuple-element.22.fields, f32[200,128]{1,0:T(8,128)S(1)} %collective-permute-done.low_halo, f32[200,128]{1,0:T(8,128)S(1)} %collective-permute-done.1.high_halo, f32[16,128]{1,0:T(8,128)S(1)} %get-tuple-element.25.metric, ...), custom_call_target="tpu_custom_call" | custom-call | flops 8388608 | bytes 8388608 | tf_op jit(solution)/shard_map/interior/pallas_call | solution.py:443
  13.4 0.0 collective-permute-done.2.on_chip
  13.5 1.6 %collective-permute-done.3.off_chip = f32[40,128]{1,0:T(8,128)S(1)} collective-permute-done((f32[40,128]{1,0:T(8,128)S(1)}, f32[40,128]{1,0:T(8,128)S(1)}, u32[]{:S(2)}, u32[]{:S(2)}) %collective-permute-start.3) | collective-permute-done | bytes 20512 | tf_op jit(solution)/shard_map/ppermute | solution.py:494
  15.1 0.5 %finish_forward.1 = (f32[2,4,16,128]{3,2,1,0:T(8,128)S(1)}, f32[2,2,16,128]{3,2,1,0:T(8,128)S(1)}) custom-call(f32[64,4,16,128]{3,2,1,0:T(8,128)S(1)} %get-tuple-element.28.done.before, f32[80,128]{1,0:T(8,128)S(1)} %get-tuple-element.29.edges, f32[8,128]{1,0:T(8,128)S(1)} %get-tuple-element.31.ends, f32[40,128]{1,0:T(8,128)S(1)} %collective-permute-done.2.on_chip, ...), custom_call_target="tpu_custom_call" | custom-call | tf_op jit(solution)/shard_map/finish_forward/pallas_call | solution.py:443
  15.6 0.6 %collective-permute-start.4 = (f32[2,4,16,128]{3,2,1,0:T(8,128)S(1)}, f32[2,4,16,128]{3,2,1,0:T(8,128)S(1)}, u32[]{:S(2)}, u32[]{:S(2)}) collective-permute-start(f32[2,4,16,128]{3,2,1,0:T(8,128)S(1)} %get-tuple-element.38.mine), channel_id=1, source_target_pairs={{0,1},{1,0},{2,3},{3,2},{4,5},{5,4},{6,7},{7,6},{8,9},{9,8},{10,11... | collective-permute-start | bytes 196616 | tf_op jit(solution)/shard_map/ppermute | solution.py:512
  16.3 0.6 %settle.1.done = f32[64,4,16,128]{3,2,1,0:T(8,128)S(1)} custom-call(f32[64,4,16,128]{3,2,1,0:T(8,128)S(1)} %get-tuple-element.28.done.before, f32[64,4,16,128]{3,2,1,0:T(8,128)S(1)} %get-tuple-element.26.part_a, f32[64,4,16,128]{3,2,1,0:T(8,128)S(1)} %get-tuple-element.27.part_b, ...), custom_call_target="tpu_custom_call", output_to_operand_aliasing={{}: (0, {})} | custom-call | flops 8388608 | bytes 8388608 | tf_op jit(solution)/shard_map/settle/pallas_call | solution.py:443
  16.9 4.5 %collective-permute-done.4.other = f32[2,4,16,128]{3,2,1,0:T(8,128)S(1)} collective-permute-done((f32[2,4,16,128]{3,2,1,0:T(8,128)S(1)}, f32[2,4,16,128]{3,2,1,0:T(8,128)S(1)}, u32[]{:S(2)}, u32[]{:S(2)}) %collective-permute-start.4) | collective-permute-done | bytes 65568 | tf_op jit(solution)/shard_map/ppermute | solution.py:512
  21.4 1.5 %back_substitute.1 = f32[64,4,16,128]{3,2,1,0:T(8,128)} custom-call(f32[64,4,16,128]{3,2,1,0:T(8,128)S(1)} %settle.1.done, f32[64,4,16,128]{3,2,1,0:T(8,128)S(1)} %get-tuple-element.37.part_c, f32[2,4,16,128]{3,2,1,0:T(8,128)S(1)} %get-tuple-element.38.mine, f32[2,4,16,128]{3,2,1,0:T(8,128)S(1)} %collective-permute-done.4.other), custom_call_target="tpu_custom_call" | custom-call | tf_op jit(solution)/shard_map/back_substitute/pallas_call | solution.py:523
Async XLA Ops:
  1.0 10.0 %collective-permute-start = (f32[200,128]{1,0:T(8,128)S(1)}, f32[200,128]{1,0:T(8,128)S(1)}, u32[]{:S(2)}, u32[]{:S(2)}) collective-permute-start(f32[200,128]{1,0:T(8,128)S(1)} %get-tuple-element.23), channel_id=1, source_target_pairs={{0,16},{16,32},{32,48},{48,64},{64,80},{80,96},{96,112},{112,128},... | collective-permute-start | bytes 307208 | tf_op jit(solution)/shard_map/ppermute | solution.py:473
  2.3 8.7 %collective-permute-start.1 = (f32[200,128]{1,0:T(8,128)S(1)}, f32[200,128]{1,0:T(8,128)S(1)}, u32[]{:S(2)}, u32[]{:S(2)}) collective-permute-start(f32[200,128]{1,0:T(8,128)S(1)} %get-tuple-element.24), channel_id=1, source_target_pairs={{16,0},{32,16},{48,32},{64,48},{80,64},{96,80},{112,96},{128,112},... | collective-permute-start | bytes 307208 | tf_op jit(solution)/shard_map/ppermute | solution.py:474
  11.1 2.3 %collective-permute-start.2 = (f32[40,128]{1,0:T(8,128)S(1)}, f32[40,128]{1,0:T(8,128)S(1)}, u32[]{:S(2)}, u32[]{:S(2)}) collective-permute-start(f32[40,128]{1,0:T(8,128)S(1)} %get-tuple-element.32), channel_id=1, source_target_pairs={{0,2},{2,0},{4,6},{6,4},{8,10},{10,8},{12,14},{14,12},{1,3},{3,1},... | collective-permute-start | bytes 61448 | tf_op jit(solution)/shard_map/ppermute | solution.py:495
  11.2 3.9 %collective-permute-start.3 = (f32[40,128]{1,0:T(8,128)S(1)}, f32[40,128]{1,0:T(8,128)S(1)}, u32[]{:S(2)}, u32[]{:S(2)}) collective-permute-start(f32[40,128]{1,0:T(8,128)S(1)} %get-tuple-element.33), channel_id=1, source_target_pairs={{0,16},{2,4},{4,2},{6,8},{8,6},{10,12},{12,10},{14,30},{16,0},{18,... | collective-permute-start | bytes 61448 | tf_op jit(solution)/shard_map/ppermute | solution.py:494
  15.6 5.8 %collective-permute-start.4 = (f32[2,4,16,128]{3,2,1,0:T(8,128)S(1)}, f32[2,4,16,128]{3,2,1,0:T(8,128)S(1)}, u32[]{:S(2)}, u32[]{:S(2)}) collective-permute-start(f32[2,4,16,128]{3,2,1,0:T(8,128)S(1)} %get-tuple-element.38.mine), channel_id=1, source_target_pairs={{0,1},{1,0},{2,3},{3,2},{4,5},{5,4},{6,7},{7,6},{8,9},{9,8},{10,11... | collective-permute-start | bytes 196616 | tf_op jit(solution)/shard_map/ppermute | solution.py:512

commit v4 on v3

--- a/solution.py
+++ b/solution.py
@@ -83,29 +83,64 @@
     for copy in early + [copy for group in copies for copy in group] + late:
         copy.start()
 
+    block = block_of(16)
+    half_levels = levels // 2
+
+    def step(k, carry):
+        inflow, before, kept_p, kept_v = carry
+        here = first + sign * k
+        weight = weights[here]
+        after = pair[link + sign * k]
+        p, v = fields[here, 3], fields[here, 1]
+        inverse = 1.0 / ((weight + after) + inflow)
+        pushed = after * (weight + inflow)
+        at = lax.rem(here, half_levels)
+        mine = block == at
+        kept_p = jnp.where(mine, pltpu.roll(p, 4 * at, 1), kept_p)
+        kept_v = jnp.where(mine, pltpu.roll(v, 4 * at, 1), kept_v)
+        part_a[here] = weight * inverse
+        part_b[here] = before * inverse
+        part_c[here] = after * inverse
+        return pushed * inverse, after, kept_p, kept_v
+
     for copy in early:
         copy.wait()
-    block = block_of(16)
-    for half in range(2):
-
-        def gather(i, carry):
-            kept_p, kept_v = carry
-            moved = []
-            for j in range(16):
-                at = 16 * i + j
-                level = half * (levels // 2) + at
-                moved.append(
-                    (block == at, pltpu.roll(fields[level, 3], 4 * at, 1), pltpu.roll(fields[level, 1], 4 * at, 1))
-                )
-            for mine, p, v in moved:
-                kept_p = jnp.where(mine, p, kept_p)
-                kept_v = jnp.where(mine, v, kept_v)
-            return kept_p, kept_v
-
-        kept = jnp.zeros((16, 128), f32)
-        kept_p, kept_v = lax.fori_loop(0, levels // 32, gather, (kept, kept))
-        edges[16 * half : 16 * half + 16, :] = kept_p
-        edges[32 + 16 * half : 48 + 16 * half, :] = kept_v
+    zeros = jnp.zeros((4, 16, 128), f32)
+    empty = jnp.zeros((16, 128), f32)
+    carry = (zeros, zeros, empty, empty)
+    for j in range(4):
+        if j == 0:
+            for copy in copies[0] + copies[1]:
+                copy.wait()
+        elif j < 3:
+            for copy in copies[j + 1]:
+                copy.wait()
+        start = j * chunk
+        count = chunk if j < 3 else chunk // 2
+        carry = loop(count, lambda k, c: step(start + k, c), carry, 8)
+        if j == 3:
+            for k in range(start + count, levels - 1):
+                carry = step(k, carry)
+            inflow, before, kept_p, kept_v = carry
+            here = first + sign * (levels - 1)
+            at = lax.rem(here, half_levels)
+            kept_p = jnp.where(block == at, pltpu.roll(fields[here, 3], 4 * at, 1), kept_p)
+            kept_v = jnp.where(block == at, pltpu.roll(fields[here, 1], 4 * at, 1), kept_v)
+            weight = weights[here]
+            inverse = 1.0 / (weight + inflow)
+            part_a[here] = weight * inverse
+            part_b[here] = before * inverse
+            part_c[here] = inverse
+            carry = (inflow, before, kept_p, kept_v)
+        if j % 2:
+            half = top + sign * (j // 2)
+            rows = pl.multiple_of(16 * half, 16)
+            edges[pl.ds(rows, 16), :] = carry[2]
+            edges[pl.ds(32 + rows, 16), :] = carry[3]
+            carry = (carry[0], carry[1], empty, empty)
+    outward = jnp.where(top == 0, 1.0 / pair[levels - 1], zeros)
+    resist[...] = inverse + outward
+
     own = jnp.where(block == 0, own_metric[...], 0.0)
     for shift in (4, 8, 16, 32, 64):
         own = own + pltpu.roll(own, shift, 1)
@@ -121,43 +156,6 @@
         sides[1, at : at + 16, :] = jnp.where(
             place >= 2, p, jnp.where(place == 1, pltpu.roll(v, 127, 1), pltpu.roll(own, 126, 1))
         )
-
-    def step(k, carry):
-        g, before = carry
-        here = first + sign * k
-        weight = weights[here]
-        after = pair[link + sign * k]
-        total = weight + before * g
-        inverse = 1.0 / (total + after)
-        part_a[here] = weight * inverse
-        part_b[here] = before * inverse
-        part_c[here] = after * inverse
-        return total * inverse, after
-
-    zeros = jnp.zeros((4, 16, 128), f32)
-    carry = (zeros, zeros)
-    for j in range(4):
-        if j == 0:
-            for copy in copies[0] + copies[1]:
-                copy.wait()
-        elif j < 3:
-            for copy in copies[j + 1]:
-                copy.wait()
-        count = chunk if j < 3 else chunk - 1
-        start = j * chunk
-        if count % 8 == 0:
-            carry = loop(count, lambda k, c: step(start + k, c), carry, 8)
-        else:
-            carry = loop(count, lambda k, c: step(start + k, c), carry, 5)
-    g, before = carry
-    here = first + sign * (levels - 1)
-    weight = weights[here]
-    inverse = 1.0 / (weight + before * g)
-    part_a[here] = weight * inverse
-    part_b[here] = before * inverse
-    part_c[here] = inverse
-    outward = jnp.where(top == 0, 1.0 / pair[levels - 1], zeros)
-    resist[...] = inverse + outward
     for copy in late:
         copy.wait()
 
@@ -199,7 +197,7 @@
     spread = 0.5 * step_dt * sound_sq * m * m
     slope_low = step_dt * 0.5 * low_halo[3 * levels : 3 * levels + 1, :]
     slope_high = step_dt * 0.5 * high_halo[3 * levels : 3 * levels + 1, :]
-    batch = 8
+    batch = 4
 
     def east(z):
         return pltpu.roll(z, 127, 1)
@@ -257,7 +255,7 @@
         return d
 
     zeros = jnp.zeros((16, 128), f32)
-    lax.fori_loop(0, levels // batch, several, (zeros,) * 4)
+    loop(levels // batch, several, (zeros,) * 4, 2)
 
     block = block_of(16)
 
@@ -291,7 +289,7 @@
     segment(0, segment(1, (ones, ones)))
 
 
-def finish_forward(done, edges, ends, on_chip, off_chip, reach, resist, out, fixes):
+def finish_forward(done, edges, ends, off_chip, on_chip, reach, resist, out, fixes):
     levels = done.shape[0]
     top, sign, first, link = order(levels)
     turn = lax.axis_index("gy")
@@ -353,9 +351,9 @@
         sum_v = reach[0, half] * own_v + (sum_v if half else 0.0)
         sum_p = reach[1, half] * fix_p + (sum_p if half else 0.0)
 
-    for by in (4, 8, 16, 32, 64):
-        sum_v = sum_v + shift(sum_v, by)
-        sum_p = sum_p + shift(sum_p, by)
+    for steps in ((4, 8, 12, 16, 20, 24, 28), (32, 64, 96)):
+        sum_v = sum([shift(sum_v, by) for by in steps], sum_v)
+        sum_p = sum([shift(sum_p, by) for by in steps], sum_p)
     edge = (lane >= 126) | (lane < 2)
     last = done[first + sign * (levels - 1)]
     out[0, 0] = last[0]
@@ -508,7 +506,7 @@
         [VM] * 7,
         [plain((2, 4, 16, 128)), near(edge)],
         name="finish_forward",
-    )(done, edges, ends, on_chip, off_chip, reach, resist)
+    )(done, edges, ends, off_chip, on_chip, reach, resist)
     other = lax.ppermute(mine, "gz", [(0, 1), (1, 0)])
 
     done = call(

time: 23.4 us -> 23.1 us (0.987)
  waiting for transfers between devices: 6.17 us -> 4.6 us
  starting transfers between devices: 7.56 us -> 9.09 us
    ppermute x1, waiting for transfers between devices: 1.63 us -> 0.06 us  [shards(): off_chip = lax.ppermute(off_chip, ('gx', 'gy'), swaps)]
    ppermute x1, starting transfers between devices: 0.09 us -> 1.59 us  [shards(): on_chip = lax.ppermute(on_chip, 'gy', [(j, j ^ 1) for j in range(ny)])]
where the time goes in v4:
time: 23.1 us; the launch traced here: 22.7 us
  starting transfers between devices  9.09 us (39%)
  Pallas kernels  8.91 us (39%)
  waiting for transfers between devices  4.6 us (20%)
    pallas_call x6, Pallas kernels, run(): pl.pallas_call(body, in_specs=ins, out_specs=[VM] * len(outs), out_shape=...  7.39 us
    ppermute x1, starting transfers between devices, shards(): lax.ppermute(low_side, 'gx', [((i + 1) % nx, i) for i in range(nx)])  5.38 us
    ppermute x1, waiting for transfers between devices, shards(): other = lax.ppermute(mine, 'gz', [(0, 1), (1, 0)])  4.53 us
    ppermute x1, starting transfers between devices, shards(): on_chip = lax.ppermute(on_chip, 'gy', [(j, j ^ 1) for j in range(ny)])  1.59 us
    pallas_call x1, Pallas kernels, shards(): pl.pallas_call(back_substitute, in_specs=[VM] * 4, out_specs=pl.BlockSpec...  1.52 us
    ppermute x1, starting transfers between devices, shards(): lax.ppermute(high_side, 'gx', [(i, (i + 1) % nx) for i in range(nx)])  1.36 us
    ppermute x1, starting transfers between devices, shards(): other = lax.ppermute(mine, 'gz', [(0, 1), (1, 0)])  0.67 us
  transfers between devices with their start and end apart: 5, of which 2 were waited for; matrix products, arithmetic and copies ran while one was open for 0% of the time, Pallas kernels for 26%

profile of v4, /device:TPU:16, one launch (start us, length us, event | category | flops | bytes accessed | tf_op | source)
XLA Modules:
  0.0 22.7 jit_solution(14566347305054531565)
XLA Ops:
  0.0 0.9 %pack_x.1 = (f32[200,128]{1,0:T(8,128)S(1)}, f32[200,128]{1,0:T(8,128)S(1)}) custom-call(f32[64,4,16,128]{3,2,1,0:T(8,128)} %state.3, f32[16,128]{1,0:T(8,128)} %metric.3), custom_call_target="tpu_custom_call" | custom-call | tf_op jit(solution)/shard_map/pack_x/pallas_call | solution.py:441
  1.0 1.4 %collective-permute-start = (f32[200,128]{1,0:T(8,128)S(1)}, f32[200,128]{1,0:T(8,128)S(1)}, u32[]{:S(2)}, u32[]{:S(2)}) collective-permute-start(f32[200,128]{1,0:T(8,128)S(1)} %get-tuple-element.23), channel_id=1, source_target_pairs={{0,16},{16,32},{32,48},{48,64},{64,80},{80,96},{96,112},{112,128},... | collective-permute-start | bytes 307208 | tf_op jit(solution)/shard_map/ppermute | solution.py:471
  2.3 5.4 %collective-permute-start.1 = (f32[200,128]{1,0:T(8,128)S(1)}, f32[200,128]{1,0:T(8,128)S(1)}, u32[]{:S(2)}, u32[]{:S(2)}) collective-permute-start(f32[200,128]{1,0:T(8,128)S(1)} %get-tuple-element.24), channel_id=1, source_target_pairs={{16,0},{32,16},{48,32},{64,48},{80,64},{96,80},{112,96},{128,112},... | collective-permute-start | bytes 307208 | tf_op jit(solution)/shard_map/ppermute | solution.py:472
  7.7 3.3 %factor.1 = (f32[64,4,16,128]{3,2,1,0:T(8,128)S(1)}, f32[16,128]{1,0:T(8,128)S(1)}, f32[64,4,16,128]{3,2,1,0:T(8,128)S(1)}, f32[64,4,16,128]{3,2,1,0:T(8,128)S(1...) custom-call(f32[64,4,16,128]{3,2,1,0:T(8,128)} %state.3, ...), custom_call_target="tpu_custom_call" | custom-call | flops 8388608 | bytes 8388608 | tf_op jit(solution)/shard_map/factor/pallas_call | solution.py:441
  11.0 0.0 collective-permute-done.low_halo
  11.0 0.0 collective-permute-done.1.high_halo
  11.0 0.1 pack_y.1
  11.1 0.1 collective-permute-start.2
  11.2 1.6 %collective-permute-start.3 = (f32[40,128]{1,0:T(8,128)S(1)}, f32[40,128]{1,0:T(8,128)S(1)}, u32[]{:S(2)}, u32[]{:S(2)}) collective-permute-start(f32[40,128]{1,0:T(8,128)S(1)} %get-tuple-element.33), channel_id=1, source_target_pairs={{0,2},{2,0},{4,6},{6,4},{8,10},{10,8},{12,14},{14,12},{1,3},{3,1},... | collective-permute-start | bytes 61448 | tf_op jit(solution)/shard_map/ppermute | solution.py:493
  12.8 2.1 %interior.1 = (f32[64,4,16,128]{3,2,1,0:T(8,128)S(1)}, f32[2,2,16,128]{3,2,1,0:T(8,128)S(1)}) custom-call(f32[64,4,16,128]{3,2,1,0:T(8,128)S(1)} %get-tuple-element.22.fields, f32[200,128]{1,0:T(8,128)S(1)} %collective-permute-done.low_halo, f32[200,128]{1,0:T(8,128)S(1)} %collective-permute-done.1.high_halo, f32[16,128]{1,0:T(8,128)S(1)} %get-tuple-element.25.metric, ...), custom_call_target="tpu_custom_call" | custom-call | flops 8388608 | bytes 8388608 | tf_op jit(solution)/shard_map/interior/pallas_call | solution.py:441
  14.9 0.1 collective-permute-done.2.off_chip
  15.0 0.0 collective-permute-done.3.on_chip
  15.0 0.3 %finish_forward.1 = (f32[2,4,16,128]{3,2,1,0:T(8,128)S(1)}, f32[2,2,16,128]{3,2,1,0:T(8,128)S(1)}) custom-call(f32[64,4,16,128]{3,2,1,0:T(8,128)S(1)} %get-tuple-element.28.done.before, f32[80,128]{1,0:T(8,128)S(1)} %get-tuple-element.29.edges, f32[8,128]{1,0:T(8,128)S(1)} %get-tuple-element.31.ends, f32[40,128]{1,0:T(8,128)S(1)} %collective-permute-done.2.off_chip, ...), custom_call_target="tpu_custom_call" | custom-call | tf_op jit(solution)/shard_map/finish_forward/pallas_call | solution.py:441
  15.3 0.7 %collective-permute-start.4 = (f32[2,4,16,128]{3,2,1,0:T(8,128)S(1)}, f32[2,4,16,128]{3,2,1,0:T(8,128)S(1)}, u32[]{:S(2)}, u32[]{:S(2)}) collective-permute-start(f32[2,4,16,128]{3,2,1,0:T(8,128)S(1)} %get-tuple-element.38.mine), channel_id=1, source_target_pairs={{0,1},{1,0},{2,3},{3,2},{4,5},{5,4},{6,7},{7,6},{8,9},{9,8},{10,11... | collective-permute-start | bytes 196616 | tf_op jit(solution)/shard_map/ppermute | solution.py:510
  16.0 0.6 %settle.1.done = f32[64,4,16,128]{3,2,1,0:T(8,128)S(1)} custom-call(f32[64,4,16,128]{3,2,1,0:T(8,128)S(1)} %get-tuple-element.28.done.before, f32[64,4,16,128]{3,2,1,0:T(8,128)S(1)} %get-tuple-element.26.part_a, f32[64,4,16,128]{3,2,1,0:T(8,128)S(1)} %get-tuple-element.27.part_b, ...), custom_call_target="tpu_custom_call", output_to_operand_aliasing={{}: (0, {})} | custom-call | flops 8388608 | bytes 8388608 | tf_op jit(solution)/shard_map/settle/pallas_call | solution.py:441
  16.6 4.5 %collective-permute-done.4.other = f32[2,4,16,128]{3,2,1,0:T(8,128)S(1)} collective-permute-done((f32[2,4,16,128]{3,2,1,0:T(8,128)S(1)}, f32[2,4,16,128]{3,2,1,0:T(8,128)S(1)}, u32[]{:S(2)}, u32[]{:S(2)}) %collective-permute-start.4) | collective-permute-done | bytes 65568 | tf_op jit(solution)/shard_map/ppermute | solution.py:510
  21.1 1.5 %back_substitute.1 = f32[64,4,16,128]{3,2,1,0:T(8,128)} custom-call(f32[64,4,16,128]{3,2,1,0:T(8,128)S(1)} %settle.1.done, f32[64,4,16,128]{3,2,1,0:T(8,128)S(1)} %get-tuple-element.37.part_c, f32[2,4,16,128]{3,2,1,0:T(8,128)S(1)} %get-tuple-element.38.mine, f32[2,4,16,128]{3,2,1,0:T(8,128)S(1)} %collective-permute-done.4.other), custom_call_target="tpu_custom_call" | custom-call | tf_op jit(solution)/shard_map/back_substitute/pallas_call | solution.py:521
Async XLA Ops:
  1.0 10.0 %collective-permute-start = (f32[200,128]{1,0:T(8,128)S(1)}, f32[200,128]{1,0:T(8,128)S(1)}, u32[]{:S(2)}, u32[]{:S(2)}) collective-permute-start(f32[200,128]{1,0:T(8,128)S(1)} %get-tuple-element.23), channel_id=1, source_target_pairs={{0,16},{16,32},{32,48},{48,64},{64,80},{80,96},{96,112},{112,128},... | collective-permute-start | bytes 307208 | tf_op jit(solution)/shard_map/ppermute | solution.py:471
  2.3 8.7 %collective-permute-start.1 = (f32[200,128]{1,0:T(8,128)S(1)}, f32[200,128]{1,0:T(8,128)S(1)}, u32[]{:S(2)}, u32[]{:S(2)}) collective-permute-start(f32[200,128]{1,0:T(8,128)S(1)} %get-tuple-element.24), channel_id=1, source_target_pairs={{16,0},{32,16},{48,32},{64,48},{80,64},{96,80},{112,96},{128,112},... | collective-permute-start | bytes 307208 | tf_op jit(solution)/shard_map/ppermute | solution.py:472
  11.1 3.9 %collective-permute-start.2 = (f32[40,128]{1,0:T(8,128)S(1)}, f32[40,128]{1,0:T(8,128)S(1)}, u32[]{:S(2)}, u32[]{:S(2)}) collective-permute-start(f32[40,128]{1,0:T(8,128)S(1)} %get-tuple-element.32), channel_id=1, source_target_pairs={{0,16},{2,4},{4,2},{6,8},{8,6},{10,12},{12,10},{14,30},{16,0},{18,... | collective-permute-start | bytes 61448 | tf_op jit(solution)/shard_map/ppermute | solution.py:492
  11.2 3.8 %collective-permute-start.3 = (f32[40,128]{1,0:T(8,128)S(1)}, f32[40,128]{1,0:T(8,128)S(1)}, u32[]{:S(2)}, u32[]{:S(2)}) collective-permute-start(f32[40,128]{1,0:T(8,128)S(1)} %get-tuple-element.33), channel_id=1, source_target_pairs={{0,2},{2,0},{4,6},{6,4},{8,10},{10,8},{12,14},{14,12},{1,3},{3,1},... | collective-permute-start | bytes 61448 | tf_op jit(solution)/shard_map/ppermute | solution.py:493
  15.3 5.8 %collective-permute-start.4 = (f32[2,4,16,128]{3,2,1,0:T(8,128)S(1)}, f32[2,4,16,128]{3,2,1,0:T(8,128)S(1)}, u32[]{:S(2)}, u32[]{:S(2)}) collective-permute-start(f32[2,4,16,128]{3,2,1,0:T(8,128)S(1)} %get-tuple-element.38.mine), channel_id=1, source_target_pairs={{0,1},{1,0},{2,3},{3,2},{4,5},{5,4},{6,7},{7,6},{8,9},{9,8},{10,11... | collective-permute-start | bytes 196616 | tf_op jit(solution)/shard_map/ppermute | solution.py:510

commit v5 on v4

--- a/solution.py
+++ b/solution.py
@@ -117,7 +117,7 @@
                 copy.wait()
         start = j * chunk
         count = chunk if j < 3 else chunk // 2
-        carry = loop(count, lambda k, c: step(start + k, c), carry, 8)
+        carry = loop(count, lambda k, c: step(start + k, c), carry, count)
         if j == 3:
             for k in range(start + count, levels - 1):
                 carry = step(k, carry)
@@ -195,9 +195,12 @@
     m = metric[...]
     slope = step_dt * 0.5 * m
     spread = 0.5 * step_dt * sound_sq * m * m
+    spread_first, spread_last = spread[0:1], spread[15:16]
+    spread_below, spread_above = pltpu.roll(spread, 1, 0), pltpu.roll(spread, 15, 0)
+    spread_west, spread_east = pltpu.roll(spread, 1, 1), pltpu.roll(spread, 127, 1)
     slope_low = step_dt * 0.5 * low_halo[3 * levels : 3 * levels + 1, :]
     slope_high = step_dt * 0.5 * high_halo[3 * levels : 3 * levels + 1, :]
-    batch = 4
+    batch = 16
 
     def east(z):
         return pltpu.roll(z, 127, 1)
@@ -236,17 +239,20 @@
             before = below(p, near_low)
             after = above(p, near_high)
             sides = before + after
-            outer = below(before, far_low) + above(after, far_high)
             p_east, p_west = east(p), west(p)
             u1 = u - slope * (after - before)
             v1 = v - slope * (p_east - p_west)
             u1_low = u_low - slope_low * (p[0:1] - far_low)
             u1_high = u_high - slope_high * (far_high - p[15:16])
-            diff_u = above(u1, u1_high) - below(u1, u1_low)
-            diff_v = east(v1) - west(v1)
-            inner = (p_east + p_west) + 2.0 * sides - 8.0 * p
-            second = outer + (east(inner) + west(inner)) - 8.0 * sides + 18.0 * p
-            p1 = p - spread * (diff_u + diff_v) - hyper_nu * second
+            inner = hyper_nu * ((p_east + p_west) + 2.0 * sides - 8.0 * p)
+            p1 = (
+                (1.0 - 18.0 * hyper_nu) * p
+                + 8.0 * hyper_nu * sides
+                - above(u1 * spread_below + hyper_nu * after, u1_high * spread_last + hyper_nu * far_high)
+                + below(u1 * spread_above - hyper_nu * before, u1_low * spread_first - hyper_nu * far_low)
+                - east(v1 * spread_west + inner)
+                + west(v1 * spread_east - inner)
+            )
             results.append(([a[f] * z for f, z in enumerate((u1, v1, w, p1))], b))
         for l, (drive, b) in zip(ls, results):
             d = tuple(drive[f] + b[f] * d[f] for f in range(4))
@@ -255,7 +261,7 @@
         return d
 
     zeros = jnp.zeros((16, 128), f32)
-    loop(levels // batch, several, (zeros,) * 4, 2)
+    loop(levels // batch, several, (zeros,) * 4, 1)
 
     block = block_of(16)
 
@@ -418,8 +424,8 @@
 
     for j in range(8):
         ks = list(range(j * chunk + (j == 0), (j + 1) * chunk))
-        for i in range(0, len(ks), 2):
-            x = several(ks[i : i + 2], x)
+        for i in range(0, len(ks), 4):
+            x = several(ks[i : i + 4], x)
         at = pl.ds((1 - top) * (levels - chunk) - sign * (j * chunk), chunk)
         copy = pltpu.make_async_copy(x_ref.at[at], out.at[at], sems.at[j])
         copy.start()

time: 23.1 us -> 22.9 us (level)
  Pallas kernels: 8.91 us -> 8.29 us
  waiting for transfers between devices: 4.6 us -> 5.08 us
    pallas_call x6, Pallas kernels: 7.39 us -> 6.77 us  [run(): pl.pallas_call(body, in_specs=ins, out_specs=[VM] * len(outs), out_shape=...]
    ppermute x1, waiting for transfers between devices: 0.06 us -> 0.54 us  [shards(): off_chip = lax.ppermute(off_chip, ('gx', 'gy'), swaps)]
  transfers between devices with their start and end apart: 5 -> 5, of which waited for: 2 -> 2; matrix products, arithmetic and copies ran while one was open for 0% -> 0% of each run, Pallas kernels for 26% -> 24%
where the time goes in v5:
time: 22.9 us; the launch traced here: 22.5 us
  starting transfers between devices  9.09 us (40%)
  Pallas kernels  8.29 us (36%)
  waiting for transfers between devices  5.08 us (22%)
    pallas_call x6, Pallas kernels, run(): pl.pallas_call(body, in_specs=ins, out_specs=[VM] * len(outs), out_shape=...  6.77 us
    ppermute x1, starting transfers between devices, shards(): lax.ppermute(low_side, 'gx', [((i + 1) % nx, i) for i in range(nx)])  5.38 us
    ppermute x1, waiting for transfers between devices, shards(): other = lax.ppermute(mine, 'gz', [(0, 1), (1, 0)])  4.54 us
    ppermute x1, starting transfers between devices, shards(): on_chip = lax.ppermute(on_chip, 'gy', [(j, j ^ 1) for j in range(ny)])  1.59 us
    pallas_call x1, Pallas kernels, shards(): pl.pallas_call(back_substitute, in_specs=[VM] * 4, out_specs=pl.BlockSpec...  1.52 us
    ppermute x1, starting transfers between devices, shards(): lax.ppermute(high_side, 'gx', [(i, (i + 1) % nx) for i in range(nx)])  1.36 us
    ppermute x1, starting transfers between devices, shards(): other = lax.ppermute(mine, 'gz', [(0, 1), (1, 0)])  0.66 us
    ppermute x1, waiting for transfers between devices, shards(): off_chip = lax.ppermute(off_chip, ('gx', 'gy'), swaps)  0.54 us
  transfers between devices with their start and end apart: 5, of which 2 were waited for; matrix products, arithmetic and copies ran while one was open for 0% of the time, Pallas kernels for 24%

profile of v5, /device:TPU:16, one launch (start us, length us, event | category | flops | bytes accessed | tf_op | source)
XLA Modules:
  0.0 22.5 jit_solution(15624745309032635242)
XLA Ops:
  0.0 0.9 %pack_x.1 = (f32[200,128]{1,0:T(8,128)S(1)}, f32[200,128]{1,0:T(8,128)S(1)}) custom-call(f32[64,4,16,128]{3,2,1,0:T(8,128)} %state.3, f32[16,128]{1,0:T(8,128)} %metric.3), custom_call_target="tpu_custom_call" | custom-call | tf_op jit(solution)/shard_map/pack_x/pallas_call | solution.py:447
  1.0 1.4 %collective-permute-start = (f32[200,128]{1,0:T(8,128)S(1)}, f32[200,128]{1,0:T(8,128)S(1)}, u32[]{:S(2)}, u32[]{:S(2)}) collective-permute-start(f32[200,128]{1,0:T(8,128)S(1)} %get-tuple-element.23), channel_id=1, source_target_pairs={{0,16},{16,32},{32,48},{48,64},{64,80},{80,96},{96,112},{112,128},... | collective-permute-start | bytes 307208 | tf_op jit(solution)/shard_map/ppermute | solution.py:477
  2.3 5.4 %collective-permute-start.1 = (f32[200,128]{1,0:T(8,128)S(1)}, f32[200,128]{1,0:T(8,128)S(1)}, u32[]{:S(2)}, u32[]{:S(2)}) collective-permute-start(f32[200,128]{1,0:T(8,128)S(1)} %get-tuple-element.24), channel_id=1, source_target_pairs={{16,0},{32,16},{48,32},{64,48},{80,64},{96,80},{112,96},{128,112},... | collective-permute-start | bytes 307208 | tf_op jit(solution)/shard_map/ppermute | solution.py:478
  7.7 3.1 %factor.1 = (f32[64,4,16,128]{3,2,1,0:T(8,128)S(1)}, f32[16,128]{1,0:T(8,128)S(1)}, f32[64,4,16,128]{3,2,1,0:T(8,128)S(1)}, f32[64,4,16,128]{3,2,1,0:T(8,128)S(1...) custom-call(f32[64,4,16,128]{3,2,1,0:T(8,128)} %state.3, ...), custom_call_target="tpu_custom_call" | custom-call | flops 8388608 | bytes 8388608 | tf_op jit(solution)/shard_map/factor/pallas_call | solution.py:447
  10.8 0.0 collective-permute-done.low_halo
  10.8 0.0 collective-permute-done.1.high_halo
  10.8 0.1 pack_y.1
  11.0 0.1 collective-permute-start.2
  11.1 1.6 %collective-permute-start.3 = (f32[40,128]{1,0:T(8,128)S(1)}, f32[40,128]{1,0:T(8,128)S(1)}, u32[]{:S(2)}, u32[]{:S(2)}) collective-permute-start(f32[40,128]{1,0:T(8,128)S(1)} %get-tuple-element.33), channel_id=1, source_target_pairs={{0,2},{2,0},{4,6},{6,4},{8,10},{10,8},{12,14},{14,12},{1,3},{3,1},... | collective-permute-start | bytes 61448 | tf_op jit(solution)/shard_map/ppermute | solution.py:499
  12.7 1.6 %interior.1 = (f32[64,4,16,128]{3,2,1,0:T(8,128)S(1)}, f32[2,2,16,128]{3,2,1,0:T(8,128)S(1)}) custom-call(f32[64,4,16,128]{3,2,1,0:T(8,128)S(1)} %get-tuple-element.22.fields, f32[200,128]{1,0:T(8,128)S(1)} %collective-permute-done.low_halo, f32[200,128]{1,0:T(8,128)S(1)} %collective-permute-done.1.high_halo, f32[16,128]{1,0:T(8,128)S(1)} %get-tuple-element.25.metric, ...), custom_call_target="tpu_custom_call" | custom-call | flops 8388608 | bytes 8388608 | tf_op jit(solution)/shard_map/interior/pallas_call | solution.py:447
  14.3 0.5 %collective-permute-done.2.off_chip = f32[40,128]{1,0:T(8,128)S(1)} collective-permute-done((f32[40,128]{1,0:T(8,128)S(1)}, f32[40,128]{1,0:T(8,128)S(1)}, u32[]{:S(2)}, u32[]{:S(2)}) %collective-permute-start.2) | collective-permute-done | bytes 20512 | tf_op jit(solution)/shard_map/ppermute | solution.py:498
  14.9 0.0 collective-permute-done.3.on_chip
  14.9 0.3 %finish_forward.1 = (f32[2,4,16,128]{3,2,1,0:T(8,128)S(1)}, f32[2,2,16,128]{3,2,1,0:T(8,128)S(1)}) custom-call(f32[64,4,16,128]{3,2,1,0:T(8,128)S(1)} %get-tuple-element.28.done.before, f32[80,128]{1,0:T(8,128)S(1)} %get-tuple-element.29.edges, f32[8,128]{1,0:T(8,128)S(1)} %get-tuple-element.31.ends, f32[40,128]{1,0:T(8,128)S(1)} %collective-permute-done.2.off_chip, ...), custom_call_target="tpu_custom_call" | custom-call | tf_op jit(solution)/shard_map/finish_forward/pallas_call | solution.py:447
  15.2 0.7 %collective-permute-start.4 = (f32[2,4,16,128]{3,2,1,0:T(8,128)S(1)}, f32[2,4,16,128]{3,2,1,0:T(8,128)S(1)}, u32[]{:S(2)}, u32[]{:S(2)}) collective-permute-start(f32[2,4,16,128]{3,2,1,0:T(8,128)S(1)} %get-tuple-element.38.mine), channel_id=1, source_target_pairs={{0,1},{1,0},{2,3},{3,2},{4,5},{5,4},{6,7},{7,6},{8,9},{9,8},{10,11... | collective-permute-start | bytes 196616 | tf_op jit(solution)/shard_map/ppermute | solution.py:516
  15.9 0.6 %settle.1.done = f32[64,4,16,128]{3,2,1,0:T(8,128)S(1)} custom-call(f32[64,4,16,128]{3,2,1,0:T(8,128)S(1)} %get-tuple-element.28.done.before, f32[64,4,16,128]{3,2,1,0:T(8,128)S(1)} %get-tuple-element.26.part_a, f32[64,4,16,128]{3,2,1,0:T(8,128)S(1)} %get-tuple-element.27.part_b, ...), custom_call_target="tpu_custom_call", output_to_operand_aliasing={{}: (0, {})} | custom-call | flops 8388608 | bytes 8388608 | tf_op jit(solution)/shard_map/settle/pallas_call | solution.py:447
  16.5 4.5 %collective-permute-done.4.other = f32[2,4,16,128]{3,2,1,0:T(8,128)S(1)} collective-permute-done((f32[2,4,16,128]{3,2,1,0:T(8,128)S(1)}, f32[2,4,16,128]{3,2,1,0:T(8,128)S(1)}, u32[]{:S(2)}, u32[]{:S(2)}) %collective-permute-start.4) | collective-permute-done | bytes 65568 | tf_op jit(solution)/shard_map/ppermute | solution.py:516
  21.0 1.5 %back_substitute.1 = f32[64,4,16,128]{3,2,1,0:T(8,128)} custom-call(f32[64,4,16,128]{3,2,1,0:T(8,128)S(1)} %settle.1.done, f32[64,4,16,128]{3,2,1,0:T(8,128)S(1)} %get-tuple-element.37.part_c, f32[2,4,16,128]{3,2,1,0:T(8,128)S(1)} %get-tuple-element.38.mine, f32[2,4,16,128]{3,2,1,0:T(8,128)S(1)} %collective-permute-done.4.other), custom_call_target="tpu_custom_call" | custom-call | tf_op jit(solution)/shard_map/back_substitute/pallas_call | solution.py:527
Async XLA Ops:
  1.0 9.9 %collective-permute-start = (f32[200,128]{1,0:T(8,128)S(1)}, f32[200,128]{1,0:T(8,128)S(1)}, u32[]{:S(2)}, u32[]{:S(2)}) collective-permute-start(f32[200,128]{1,0:T(8,128)S(1)} %get-tuple-element.23), channel_id=1, source_target_pairs={{0,16},{16,32},{32,48},{48,64},{64,80},{80,96},{96,112},{112,128},... | collective-permute-start | bytes 307208 | tf_op jit(solution)/shard_map/ppermute | solution.py:477
  2.3 8.5 %collective-permute-start.1 = (f32[200,128]{1,0:T(8,128)S(1)}, f32[200,128]{1,0:T(8,128)S(1)}, u32[]{:S(2)}, u32[]{:S(2)}) collective-permute-start(f32[200,128]{1,0:T(8,128)S(1)} %get-tuple-element.24), channel_id=1, source_target_pairs={{16,0},{32,16},{48,32},{64,48},{80,64},{96,80},{112,96},{128,112},... | collective-permute-start | bytes 307208 | tf_op jit(solution)/shard_map/ppermute | solution.py:478
  11.0 3.9 %collective-permute-start.2 = (f32[40,128]{1,0:T(8,128)S(1)}, f32[40,128]{1,0:T(8,128)S(1)}, u32[]{:S(2)}, u32[]{:S(2)}) collective-permute-start(f32[40,128]{1,0:T(8,128)S(1)} %get-tuple-element.32), channel_id=1, source_target_pairs={{0,16},{2,4},{4,2},{6,8},{8,6},{10,12},{12,10},{14,30},{16,0},{18,... | collective-permute-start | bytes 61448 | tf_op jit(solution)/shard_map/ppermute | solution.py:498
  11.1 3.8 %collective-permute-start.3 = (f32[40,128]{1,0:T(8,128)S(1)}, f32[40,128]{1,0:T(8,128)S(1)}, u32[]{:S(2)}, u32[]{:S(2)}) collective-permute-start(f32[40,128]{1,0:T(8,128)S(1)} %get-tuple-element.33), channel_id=1, source_target_pairs={{0,2},{2,0},{4,6},{6,4},{8,10},{10,8},{12,14},{14,12},{1,3},{3,1},... | collective-permute-start | bytes 61448 | tf_op jit(solution)/shard_map/ppermute | solution.py:499
  15.2 5.8 %collective-permute-start.4 = (f32[2,4,16,128]{3,2,1,0:T(8,128)S(1)}, f32[2,4,16,128]{3,2,1,0:T(8,128)S(1)}, u32[]{:S(2)}, u32[]{:S(2)}) collective-permute-start(f32[2,4,16,128]{3,2,1,0:T(8,128)S(1)} %get-tuple-element.38.mine), channel_id=1, source_target_pairs={{0,1},{1,0},{2,3},{3,2},{4,5},{5,4},{6,7},{7,6},{8,9},{9,8},{10,11... | collective-permute-start | bytes 196616 | tf_op jit(solution)/shard_map/ppermute | solution.py:516

commit v6 on v5

--- a/solution.py
+++ b/solution.py
@@ -45,10 +45,10 @@
 def pack_x(state, metric, low_side, high_side, sems):
     levels = state.shape[0]
     copies = []
-    for out, rows in ((low_side, (0, 1, 0)), (high_side, (15, 14, 15))):
-        for part, (field, row) in enumerate(zip((3, 3, 0), rows)):
-            copies.append((state.at[:, field, row], out.at[pl.ds(part * levels, levels)]))
-        copies.append((metric.at[pl.ds(rows[0], 1)], out.at[pl.ds(3 * levels, 1)]))
+    for out, pair, row in ((low_side, 0, 0), (high_side, 14, 15)):
+        copies.append((state.at[:, 3, pl.ds(pair, 2)], out.at[pl.ds(0, 2 * levels)].reshape(levels, 2, 128)))
+        copies.append((state.at[:, 0, row], out.at[pl.ds(2 * levels, levels)]))
+        copies.append((metric.at[pl.ds(row, 1)], out.at[pl.ds(3 * levels, 1)]))
     copies = [pltpu.make_async_copy(src, dst, sems.at[i]) for i, (src, dst) in enumerate(copies)]
     for copy in copies:
         copy.start()
@@ -172,8 +172,8 @@
             for j in range(32):
                 at = 32 * i + j
                 level = half * (levels // 2) + at
-                low = jnp.broadcast_to(low_halo[pl.ds(level, 1), :], (8, 128))
-                high = jnp.broadcast_to(high_halo[pl.ds(level, 1), :], (8, 128))
+                low = jnp.broadcast_to(low_halo[pl.ds(2 * level + 1, 1), :], (8, 128))
+                high = jnp.broadcast_to(high_halo[pl.ds(2 * level, 1), :], (8, 128))
                 both = pltpu.roll(jnp.where(row == 2 * half, low, high), 4 * at, 1)
                 moved.append(((block == at) & (row // 2 == half), both))
             for mine, both in moved:
@@ -223,11 +223,11 @@
                     fields[l, 3],
                     fields[l, 0],
                     fields[l, 1],
-                    low_halo[pl.ds(l, 1), :],
-                    low_halo[pl.ds(levels + l, 1), :],
+                    low_halo[pl.ds(2 * l + 1, 1), :],
+                    low_halo[pl.ds(2 * l, 1), :],
                     low_halo[pl.ds(2 * levels + l, 1), :],
-                    high_halo[pl.ds(l, 1), :],
-                    high_halo[pl.ds(levels + l, 1), :],
+                    high_halo[pl.ds(2 * l, 1), :],
+                    high_halo[pl.ds(2 * l + 1, 1), :],
                     high_halo[pl.ds(2 * levels + l, 1), :],
                     [part_a[l, f] for f in range(4)],
                     [part_b[l, f] for f in range(4)],
@@ -472,7 +472,7 @@
     state, metric, couple, base = far(state), far(metric), far(couple), far(base)
 
     low_side, high_side = call(
-        pack_x, [HB, HB], [plain(side), plain(side)], [dma((8,))], name="pack_x"
+        pack_x, [HB, HB], [plain(side), plain(side)], [dma((6,))], name="pack_x"
     )(state, metric)
     low_halo = lax.ppermute(high_side, "gx", [(i, (i + 1) % nx) for i in range(nx)])
     high_halo = lax.ppermute(low_side, "gx", [((i + 1) % nx, i) for i in range(nx)])

time: 22.9 us -> 22.9 us (level)
  no operation moved by 1% of the time
where the time goes in v6:
time: 22.9 us; the launch traced here: 22.6 us
  starting transfers between devices  9.09 us (40%)
  Pallas kernels  8.33 us (36%)
  waiting for transfers between devices  5.07 us (22%)
    pallas_call x6, Pallas kernels, run(): pl.pallas_call(body, in_specs=ins, out_specs=[VM] * len(outs), out_shape=...  6.81 us
    ppermute x1, starting transfers between devices, shards(): lax.ppermute(low_side, 'gx', [((i + 1) % nx, i) for i in range(nx)])  5.38 us
    ppermute x1, waiting for transfers between devices, shards(): other = lax.ppermute(mine, 'gz', [(0, 1), (1, 0)])  4.54 us
    ppermute x1, starting transfers between devices, shards(): on_chip = lax.ppermute(on_chip, 'gy', [(j, j ^ 1) for j in range(ny)])  1.59 us
    pallas_call x1, Pallas kernels, shards(): pl.pallas_call(back_substitute, in_specs=[VM] * 4, out_specs=pl.BlockSpec...  1.52 us
    ppermute x1, starting transfers between devices, shards(): lax.ppermute(high_side, 'gx', [(i, (i + 1) % nx) for i in range(nx)])  1.36 us
    ppermute x1, starting transfers between devices, shards(): other = lax.ppermute(mine, 'gz', [(0, 1), (1, 0)])  0.66 us
    ppermute x1, waiting for transfers between devices, shards(): off_chip = lax.ppermute(off_chip, ('gx', 'gy'), swaps)  0.52 us
  transfers between devices with their start and end apart: 5, of which 2 were waited for; matrix products, arithmetic and copies ran while one was open for 0% of the time, Pallas kernels for 24%

profile of v6, /device:TPU:16, one launch (start us, length us, event | category | flops | bytes accessed | tf_op | source)
XLA Modules:
  0.0 22.6 jit_solution(3041486269671200714)
XLA Ops:
  0.0 1.0 %pack_x.1 = (f32[200,128]{1,0:T(8,128)S(1)}, f32[200,128]{1,0:T(8,128)S(1)}) custom-call(f32[64,4,16,128]{3,2,1,0:T(8,128)} %state.3, f32[16,128]{1,0:T(8,128)} %metric.3), custom_call_target="tpu_custom_call" | custom-call | tf_op jit(solution)/shard_map/pack_x/pallas_call | solution.py:447
  1.0 1.4 %collective-permute-start = (f32[200,128]{1,0:T(8,128)S(1)}, f32[200,128]{1,0:T(8,128)S(1)}, u32[]{:S(2)}, u32[]{:S(2)}) collective-permute-start(f32[200,128]{1,0:T(8,128)S(1)} %get-tuple-element.23), channel_id=1, source_target_pairs={{0,16},{16,32},{32,48},{48,64},{64,80},{80,96},{96,112},{112,128},... | collective-permute-start | bytes 307208 | tf_op jit(solution)/shard_map/ppermute | solution.py:477
  2.3 5.4 %collective-permute-start.1 = (f32[200,128]{1,0:T(8,128)S(1)}, f32[200,128]{1,0:T(8,128)S(1)}, u32[]{:S(2)}, u32[]{:S(2)}) collective-permute-start(f32[200,128]{1,0:T(8,128)S(1)} %get-tuple-element.24), channel_id=1, source_target_pairs={{16,0},{32,16},{48,32},{64,48},{80,64},{96,80},{112,96},{128,112},... | collective-permute-start | bytes 307208 | tf_op jit(solution)/shard_map/ppermute | solution.py:478
  7.7 3.1 %factor.1 = (f32[64,4,16,128]{3,2,1,0:T(8,128)S(1)}, f32[16,128]{1,0:T(8,128)S(1)}, f32[64,4,16,128]{3,2,1,0:T(8,128)S(1)}, f32[64,4,16,128]{3,2,1,0:T(8,128)S(1...) custom-call(f32[64,4,16,128]{3,2,1,0:T(8,128)} %state.3, ...), custom_call_target="tpu_custom_call" | custom-call | flops 8388608 | bytes 8388608 | tf_op jit(solution)/shard_map/factor/pallas_call | solution.py:447
  10.8 0.0 collective-permute-done.low_halo
  10.9 0.0 collective-permute-done.1.high_halo
  10.9 0.1 pack_y.1
  11.0 0.1 collective-permute-start.2
  11.1 1.6 %collective-permute-start.3 = (f32[40,128]{1,0:T(8,128)S(1)}, f32[40,128]{1,0:T(8,128)S(1)}, u32[]{:S(2)}, u32[]{:S(2)}) collective-permute-start(f32[40,128]{1,0:T(8,128)S(1)} %get-tuple-element.33), channel_id=1, source_target_pairs={{0,2},{2,0},{4,6},{6,4},{8,10},{10,8},{12,14},{14,12},{1,3},{3,1},... | collective-permute-start | bytes 61448 | tf_op jit(solution)/shard_map/ppermute | solution.py:499
  12.7 1.7 %interior.1 = (f32[64,4,16,128]{3,2,1,0:T(8,128)S(1)}, f32[2,2,16,128]{3,2,1,0:T(8,128)S(1)}) custom-call(f32[64,4,16,128]{3,2,1,0:T(8,128)S(1)} %get-tuple-element.22.fields, f32[200,128]{1,0:T(8,128)S(1)} %collective-permute-done.low_halo, f32[200,128]{1,0:T(8,128)S(1)} %collective-permute-done.1.high_halo, f32[16,128]{1,0:T(8,128)S(1)} %get-tuple-element.25.metric, ...), custom_call_target="tpu_custom_call" | custom-call | flops 8388608 | bytes 8388608 | tf_op jit(solution)/shard_map/interior/pallas_call | solution.py:447
  14.4 0.5 %collective-permute-done.2.off_chip = f32[40,128]{1,0:T(8,128)S(1)} collective-permute-done((f32[40,128]{1,0:T(8,128)S(1)}, f32[40,128]{1,0:T(8,128)S(1)}, u32[]{:S(2)}, u32[]{:S(2)}) %collective-permute-start.2) | collective-permute-done | bytes 20512 | tf_op jit(solution)/shard_map/ppermute | solution.py:498
  14.9 0.0 collective-permute-done.3.on_chip
  14.9 0.3 %finish_forward.1 = (f32[2,4,16,128]{3,2,1,0:T(8,128)S(1)}, f32[2,2,16,128]{3,2,1,0:T(8,128)S(1)}) custom-call(f32[64,4,16,128]{3,2,1,0:T(8,128)S(1)} %get-tuple-element.28.done.before, f32[80,128]{1,0:T(8,128)S(1)} %get-tuple-element.29.edges, f32[8,128]{1,0:T(8,128)S(1)} %get-tuple-element.31.ends, f32[40,128]{1,0:T(8,128)S(1)} %collective-permute-done.2.off_chip, ...), custom_call_target="tpu_custom_call" | custom-call | tf_op jit(solution)/shard_map/finish_forward/pallas_call | solution.py:447
  15.2 0.7 %collective-permute-start.4 = (f32[2,4,16,128]{3,2,1,0:T(8,128)S(1)}, f32[2,4,16,128]{3,2,1,0:T(8,128)S(1)}, u32[]{:S(2)}, u32[]{:S(2)}) collective-permute-start(f32[2,4,16,128]{3,2,1,0:T(8,128)S(1)} %get-tuple-element.38.mine), channel_id=1, source_target_pairs={{0,1},{1,0},{2,3},{3,2},{4,5},{5,4},{6,7},{7,6},{8,9},{9,8},{10,11... | collective-permute-start | bytes 196616 | tf_op jit(solution)/shard_map/ppermute | solution.py:516
  15.9 0.6 %settle.1.done = f32[64,4,16,128]{3,2,1,0:T(8,128)S(1)} custom-call(f32[64,4,16,128]{3,2,1,0:T(8,128)S(1)} %get-tuple-element.28.done.before, f32[64,4,16,128]{3,2,1,0:T(8,128)S(1)} %get-tuple-element.26.part_a, f32[64,4,16,128]{3,2,1,0:T(8,128)S(1)} %get-tuple-element.27.part_b, ...), custom_call_target="tpu_custom_call", output_to_operand_aliasing={{}: (0, {})} | custom-call | flops 8388608 | bytes 8388608 | tf_op jit(solution)/shard_map/settle/pallas_call | solution.py:447
  16.5 4.5 %collective-permute-done.4.other = f32[2,4,16,128]{3,2,1,0:T(8,128)S(1)} collective-permute-done((f32[2,4,16,128]{3,2,1,0:T(8,128)S(1)}, f32[2,4,16,128]{3,2,1,0:T(8,128)S(1)}, u32[]{:S(2)}, u32[]{:S(2)}) %collective-permute-start.4) | collective-permute-done | bytes 65568 | tf_op jit(solution)/shard_map/ppermute | solution.py:516
  21.0 1.5 %back_substitute.1 = f32[64,4,16,128]{3,2,1,0:T(8,128)} custom-call(f32[64,4,16,128]{3,2,1,0:T(8,128)S(1)} %settle.1.done, f32[64,4,16,128]{3,2,1,0:T(8,128)S(1)} %get-tuple-element.37.part_c, f32[2,4,16,128]{3,2,1,0:T(8,128)S(1)} %get-tuple-element.38.mine, f32[2,4,16,128]{3,2,1,0:T(8,128)S(1)} %collective-permute-done.4.other), custom_call_target="tpu_custom_call" | custom-call | tf_op jit(solution)/shard_map/back_substitute/pallas_call | solution.py:527
Async XLA Ops:
  1.0 9.9 %collective-permute-start = (f32[200,128]{1,0:T(8,128)S(1)}, f32[200,128]{1,0:T(8,128)S(1)}, u32[]{:S(2)}, u32[]{:S(2)}) collective-permute-start(f32[200,128]{1,0:T(8,128)S(1)} %get-tuple-element.23), channel_id=1, source_target_pairs={{0,16},{16,32},{32,48},{48,64},{64,80},{80,96},{96,112},{112,128},... | collective-permute-start | bytes 307208 | tf_op jit(solution)/shard_map/ppermute | solution.py:477
  2.3 8.5 %collective-permute-start.1 = (f32[200,128]{1,0:T(8,128)S(1)}, f32[200,128]{1,0:T(8,128)S(1)}, u32[]{:S(2)}, u32[]{:S(2)}) collective-permute-start(f32[200,128]{1,0:T(8,128)S(1)} %get-tuple-element.24), channel_id=1, source_target_pairs={{16,0},{32,16},{48,32},{64,48},{80,64},{96,80},{112,96},{128,112},... | collective-permute-start | bytes 307208 | tf_op jit(solution)/shard_map/ppermute | solution.py:478
  11.0 3.9 %collective-permute-start.2 = (f32[40,128]{1,0:T(8,128)S(1)}, f32[40,128]{1,0:T(8,128)S(1)}, u32[]{:S(2)}, u32[]{:S(2)}) collective-permute-start(f32[40,128]{1,0:T(8,128)S(1)} %get-tuple-element.32), channel_id=1, source_target_pairs={{0,16},{2,4},{4,2},{6,8},{8,6},{10,12},{12,10},{14,30},{16,0},{18,... | collective-permute-start | bytes 61448 | tf_op jit(solution)/shard_map/ppermute | solution.py:498
  11.1 3.8 %collective-permute-start.3 = (f32[40,128]{1,0:T(8,128)S(1)}, f32[40,128]{1,0:T(8,128)S(1)}, u32[]{:S(2)}, u32[]{:S(2)}) collective-permute-start(f32[40,128]{1,0:T(8,128)S(1)} %get-tuple-element.33), channel_id=1, source_target_pairs={{0,2},{2,0},{4,6},{6,4},{8,10},{10,8},{12,14},{14,12},{1,3},{3,1},... | collective-permute-start | bytes 61448 | tf_op jit(solution)/shard_map/ppermute | solution.py:499
  15.2 5.8 %collective-permute-start.4 = (f32[2,4,16,128]{3,2,1,0:T(8,128)S(1)}, f32[2,4,16,128]{3,2,1,0:T(8,128)S(1)}, u32[]{:S(2)}, u32[]{:S(2)}) collective-permute-start(f32[2,4,16,128]{3,2,1,0:T(8,128)S(1)} %get-tuple-element.38.mine), channel_id=1, source_target_pairs={{0,1},{1,0},{2,3},{3,2},{4,5},{5,4},{6,7},{7,6},{8,9},{9,8},{10,11... | collective-permute-start | bytes 196616 | tf_op jit(solution)/shard_map/ppermute | solution.py:516

commit v7 on v5

--- a/solution.py
+++ b/solution.py
@@ -424,8 +424,8 @@
 
     for j in range(8):
         ks = list(range(j * chunk + (j == 0), (j + 1) * chunk))
-        for i in range(0, len(ks), 4):
-            x = several(ks[i : i + 4], x)
+        for i in range(0, len(ks), 8):
+            x = several(ks[i : i + 8], x)
         at = pl.ds((1 - top) * (levels - chunk) - sign * (j * chunk), chunk)
         copy = pltpu.make_async_copy(x_ref.at[at], out.at[at], sems.at[j])
         copy.start()

time: 22.9 us -> 22.9 us (level)
  no operation moved by 1% of the time
where the time goes in v7:
time: 22.9 us; the launch traced here: 22.5 us
  starting transfers between devices  9.09 us (40%)
  Pallas kernels  8.29 us (36%)
  waiting for transfers between devices  5.08 us (22%)
    pallas_call x6, Pallas kernels, run(): pl.pallas_call(body, in_specs=ins, out_specs=[VM] * len(outs), out_shape=...  6.77 us
    ppermute x1, starting transfers between devices, shards(): lax.ppermute(low_side, 'gx', [((i + 1) % nx, i) for i in range(nx)])  5.38 us
    ppermute x1, waiting for transfers between devices, shards(): other = lax.ppermute(mine, 'gz', [(0, 1), (1, 0)])  4.54 us
    ppermute x1, starting transfers between devices, shards(): on_chip = lax.ppermute(on_chip, 'gy', [(j, j ^ 1) for j in range(ny)])  1.59 us
    pallas_call x1, Pallas kernels, shards(): pl.pallas_call(back_substitute, in_specs=[VM] * 4, out_specs=pl.BlockSpec...  1.52 us
    ppermute x1, starting transfers between devices, shards(): lax.ppermute(high_side, 'gx', [(i, (i + 1) % nx) for i in range(nx)])  1.36 us
    ppermute x1, starting transfers between devices, shards(): other = lax.ppermute(mine, 'gz', [(0, 1), (1, 0)])  0.66 us
    ppermute x1, waiting for transfers between devices, shards(): off_chip = lax.ppermute(off_chip, ('gx', 'gy'), swaps)  0.54 us
  transfers between devices with their start and end apart: 5, of which 2 were waited for; matrix products, arithmetic and copies ran while one was open for 0% of the time, Pallas kernels for 24%

profile of v7, /device:TPU:16, one launch (start us, length us, event | category | flops | bytes accessed | tf_op | source)
XLA Modules:
  0.0 22.5 jit_solution(15138078439215356645)
XLA Ops:
  0.0 0.9 %pack_x.1 = (f32[200,128]{1,0:T(8,128)S(1)}, f32[200,128]{1,0:T(8,128)S(1)}) custom-call(f32[64,4,16,128]{3,2,1,0:T(8,128)} %state.3, f32[16,128]{1,0:T(8,128)} %metric.3), custom_call_target="tpu_custom_call" | custom-call | tf_op jit(solution)/shard_map/pack_x/pallas_call | solution.py:447
  1.0 1.4 %collective-permute-start = (f32[200,128]{1,0:T(8,128)S(1)}, f32[200,128]{1,0:T(8,128)S(1)}, u32[]{:S(2)}, u32[]{:S(2)}) collective-permute-start(f32[200,128]{1,0:T(8,128)S(1)} %get-tuple-element.23), channel_id=1, source_target_pairs={{0,16},{16,32},{32,48},{48,64},{64,80},{80,96},{96,112},{112,128},... | collective-permute-start | bytes 307208 | tf_op jit(solution)/shard_map/ppermute | solution.py:477
  2.3 5.4 %collective-permute-start.1 = (f32[200,128]{1,0:T(8,128)S(1)}, f32[200,128]{1,0:T(8,128)S(1)}, u32[]{:S(2)}, u32[]{:S(2)}) collective-permute-start(f32[200,128]{1,0:T(8,128)S(1)} %get-tuple-element.24), channel_id=1, source_target_pairs={{16,0},{32,16},{48,32},{64,48},{80,64},{96,80},{112,96},{128,112},... | collective-permute-start | bytes 307208 | tf_op jit(solution)/shard_map/ppermute | solution.py:478
  7.7 3.1 %factor.1 = (f32[64,4,16,128]{3,2,1,0:T(8,128)S(1)}, f32[16,128]{1,0:T(8,128)S(1)}, f32[64,4,16,128]{3,2,1,0:T(8,128)S(1)}, f32[64,4,16,128]{3,2,1,0:T(8,128)S(1...) custom-call(f32[64,4,16,128]{3,2,1,0:T(8,128)} %state.3, ...), custom_call_target="tpu_custom_call" | custom-call | flops 8388608 | bytes 8388608 | tf_op jit(solution)/shard_map/factor/pallas_call | solution.py:447
  10.8 0.0 collective-permute-done.low_halo
  10.8 0.0 collective-permute-done.1.high_halo
  10.8 0.1 pack_y.1
  11.0 0.1 collective-permute-start.2
  11.1 1.6 %collective-permute-start.3 = (f32[40,128]{1,0:T(8,128)S(1)}, f32[40,128]{1,0:T(8,128)S(1)}, u32[]{:S(2)}, u32[]{:S(2)}) collective-permute-start(f32[40,128]{1,0:T(8,128)S(1)} %get-tuple-element.33), channel_id=1, source_target_pairs={{0,2},{2,0},{4,6},{6,4},{8,10},{10,8},{12,14},{14,12},{1,3},{3,1},... | collective-permute-start | bytes 61448 | tf_op jit(solution)/shard_map/ppermute | solution.py:499
  12.7 1.6 %interior.1 = (f32[64,4,16,128]{3,2,1,0:T(8,128)S(1)}, f32[2,2,16,128]{3,2,1,0:T(8,128)S(1)}) custom-call(f32[64,4,16,128]{3,2,1,0:T(8,128)S(1)} %get-tuple-element.22.fields, f32[200,128]{1,0:T(8,128)S(1)} %collective-permute-done.low_halo, f32[200,128]{1,0:T(8,128)S(1)} %collective-permute-done.1.high_halo, f32[16,128]{1,0:T(8,128)S(1)} %get-tuple-element.25.metric, ...), custom_call_target="tpu_custom_call" | custom-call | flops 8388608 | bytes 8388608 | tf_op jit(solution)/shard_map/interior/pallas_call | solution.py:447
  14.3 0.5 %collective-permute-done.2.off_chip = f32[40,128]{1,0:T(8,128)S(1)} collective-permute-done((f32[40,128]{1,0:T(8,128)S(1)}, f32[40,128]{1,0:T(8,128)S(1)}, u32[]{:S(2)}, u32[]{:S(2)}) %collective-permute-start.2) | collective-permute-done | bytes 20512 | tf_op jit(solution)/shard_map/ppermute | solution.py:498
  14.9 0.0 collective-permute-done.3.on_chip
  14.9 0.3 %finish_forward.1 = (f32[2,4,16,128]{3,2,1,0:T(8,128)S(1)}, f32[2,2,16,128]{3,2,1,0:T(8,128)S(1)}) custom-call(f32[64,4,16,128]{3,2,1,0:T(8,128)S(1)} %get-tuple-element.28.done.before, f32[80,128]{1,0:T(8,128)S(1)} %get-tuple-element.29.edges, f32[8,128]{1,0:T(8,128)S(1)} %get-tuple-element.31.ends, f32[40,128]{1,0:T(8,128)S(1)} %collective-permute-done.2.off_chip, ...), custom_call_target="tpu_custom_call" | custom-call | tf_op jit(solution)/shard_map/finish_forward/pallas_call | solution.py:447
  15.2 0.7 %collective-permute-start.4 = (f32[2,4,16,128]{3,2,1,0:T(8,128)S(1)}, f32[2,4,16,128]{3,2,1,0:T(8,128)S(1)}, u32[]{:S(2)}, u32[]{:S(2)}) collective-permute-start(f32[2,4,16,128]{3,2,1,0:T(8,128)S(1)} %get-tuple-element.38.mine), channel_id=1, source_target_pairs={{0,1},{1,0},{2,3},{3,2},{4,5},{5,4},{6,7},{7,6},{8,9},{9,8},{10,11... | collective-permute-start | bytes 196616 | tf_op jit(solution)/shard_map/ppermute | solution.py:516
  15.9 0.6 %settle.1.done = f32[64,4,16,128]{3,2,1,0:T(8,128)S(1)} custom-call(f32[64,4,16,128]{3,2,1,0:T(8,128)S(1)} %get-tuple-element.28.done.before, f32[64,4,16,128]{3,2,1,0:T(8,128)S(1)} %get-tuple-element.26.part_a, f32[64,4,16,128]{3,2,1,0:T(8,128)S(1)} %get-tuple-element.27.part_b, ...), custom_call_target="tpu_custom_call", output_to_operand_aliasing={{}: (0, {})} | custom-call | flops 8388608 | bytes 8388608 | tf_op jit(solution)/shard_map/settle/pallas_call | solution.py:447
  16.5 4.5 %collective-permute-done.4.other = f32[2,4,16,128]{3,2,1,0:T(8,128)S(1)} collective-permute-done((f32[2,4,16,128]{3,2,1,0:T(8,128)S(1)}, f32[2,4,16,128]{3,2,1,0:T(8,128)S(1)}, u32[]{:S(2)}, u32[]{:S(2)}) %collective-permute-start.4) | collective-permute-done | bytes 65568 | tf_op jit(solution)/shard_map/ppermute | solution.py:516
  21.0 1.5 %back_substitute.1 = f32[64,4,16,128]{3,2,1,0:T(8,128)} custom-call(f32[64,4,16,128]{3,2,1,0:T(8,128)S(1)} %settle.1.done, f32[64,4,16,128]{3,2,1,0:T(8,128)S(1)} %get-tuple-element.37.part_c, f32[2,4,16,128]{3,2,1,0:T(8,128)S(1)} %get-tuple-element.38.mine, f32[2,4,16,128]{3,2,1,0:T(8,128)S(1)} %collective-permute-done.4.other), custom_call_target="tpu_custom_call" | custom-call | tf_op jit(solution)/shard_map/back_substitute/pallas_call | solution.py:527
Async XLA Ops:
  1.0 9.9 %collective-permute-start = (f32[200,128]{1,0:T(8,128)S(1)}, f32[200,128]{1,0:T(8,128)S(1)}, u32[]{:S(2)}, u32[]{:S(2)}) collective-permute-start(f32[200,128]{1,0:T(8,128)S(1)} %get-tuple-element.23), channel_id=1, source_target_pairs={{0,16},{16,32},{32,48},{48,64},{64,80},{80,96},{96,112},{112,128},... | collective-permute-start | bytes 307208 | tf_op jit(solution)/shard_map/ppermute | solution.py:477
  2.3 8.5 %collective-permute-start.1 = (f32[200,128]{1,0:T(8,128)S(1)}, f32[200,128]{1,0:T(8,128)S(1)}, u32[]{:S(2)}, u32[]{:S(2)}) collective-permute-start(f32[200,128]{1,0:T(8,128)S(1)} %get-tuple-element.24), channel_id=1, source_target_pairs={{16,0},{32,16},{48,32},{64,48},{80,64},{96,80},{112,96},{128,112},... | collective-permute-start | bytes 307208 | tf_op jit(solution)/shard_map/ppermute | solution.py:478
  11.0 3.9 %collective-permute-start.2 = (f32[40,128]{1,0:T(8,128)S(1)}, f32[40,128]{1,0:T(8,128)S(1)}, u32[]{:S(2)}, u32[]{:S(2)}) collective-permute-start(f32[40,128]{1,0:T(8,128)S(1)} %get-tuple-element.32), channel_id=1, source_target_pairs={{0,16},{2,4},{4,2},{6,8},{8,6},{10,12},{12,10},{14,30},{16,0},{18,... | collective-permute-start | bytes 61448 | tf_op jit(solution)/shard_map/ppermute | solution.py:498
  11.1 3.8 %collective-permute-start.3 = (f32[40,128]{1,0:T(8,128)S(1)}, f32[40,128]{1,0:T(8,128)S(1)}, u32[]{:S(2)}, u32[]{:S(2)}) collective-permute-start(f32[40,128]{1,0:T(8,128)S(1)} %get-tuple-element.33), channel_id=1, source_target_pairs={{0,2},{2,0},{4,6},{6,4},{8,10},{10,8},{12,14},{14,12},{1,3},{3,1},... | collective-permute-start | bytes 61448 | tf_op jit(solution)/shard_map/ppermute | solution.py:499
  15.2 5.8 %collective-permute-start.4 = (f32[2,4,16,128]{3,2,1,0:T(8,128)S(1)}, f32[2,4,16,128]{3,2,1,0:T(8,128)S(1)}, u32[]{:S(2)}, u32[]{:S(2)}) collective-permute-start(f32[2,4,16,128]{3,2,1,0:T(8,128)S(1)} %get-tuple-element.38.mine), channel_id=1, source_target_pairs={{0,1},{1,0},{2,3},{3,2},{4,5},{5,4},{6,7},{7,6},{8,9},{9,8},{10,11... | collective-permute-start | bytes 196616 | tf_op jit(solution)/shard_map/ppermute | solution.py:516
